TPU v7x, 32 devices: a whole 2x2x4 slice. The times are simulated.
32 devices in a mesh: dp: 16 (over z, y, x), seq: 2 (over core).
Axes of the slice: x: 2, y: 2, z: 4, core: 2. Of those that a mesh axis runs over, the one named last changes fastest.
Arguments:
- tokens: bfloat16 [16, 1536, 1024], P('dp', 'seq'), may hold values from -6 to 6
- segment_ids: int32 [16, 1536], P('dp'), may hold values from 0 to 5, never falling along the last dimension, each value on 1 to 768 neighbouring positions
- cotangent: bfloat16 [16, 1536, 1024], P('dp', 'seq'), may hold values from -6 to 6
- attention_weights: float32 [4, 1024, 1024], P(None, 'dp'), may hold values from -0.1875 to 0.1875
- feed_weights: float32 [3, 4096, 1024], P(None, 'dp'), may hold values from -0.1875 to 0.1875
- attention_scales: float32 [3, 1024], P(None, 'dp'), may hold values from 0.2 to 1.6, as said below
- feed_scales: float32 [2, 4096], P(None, 'dp'), may hold values from 0.5 to 2
- attention_first: float32 [4, 1024, 1024], P(None, 'dp'), may hold values from -8192 to 8192
- attention_second: float32 [4, 1024, 1024], P(None, 'dp'), may hold values from 235929 to 235929600
- feed_first: float32 [3, 4096, 1024], P(None, 'dp'), may hold values from -8192 to 8192
- feed_second: float32 [3, 4096, 1024], P(None, 'dp'), may hold values from 235929 to 235929600
- attention_scale_first: float32 [3, 1024], P(None, 'dp'), may hold values from -8192 to 8192
- attention_scale_second: float32 [3, 1024], P(None, 'dp'), may hold values from 235929 to 235929600
- feed_scale_first: float32 [2, 4096], P(None, 'dp'), may hold values from -8192 to 8192
- feed_scale_second: float32 [2, 4096], P(None, 'dp'), may hold values from 235929 to 235929600
Outputs:
- output: float32 [16, 1536, 1024], P('dp', 'seq')
- input_grad: float32 [16, 1536, 1024], P('dp', 'seq')
- attention_grad: float32 [4, 1024, 1024], P(None, 'dp')
- feed_grad: float32 [3, 4096, 1024], P(None, 'dp')
- attention_scale_grad: float32 [3, 1024], P(None, 'dp')
- feed_scale_grad: float32 [2, 4096], P(None, 'dp')
- attention_change: float32 [4, 1024, 1024], P(None, 'dp')
- feed_change: float32 [3, 4096, 1024], P(None, 'dp')
- attention_scale_change: float32 [3, 1024], P(None, 'dp')
- feed_scale_change: float32 [2, 4096], P(None, 'dp')
Inputs may be any that keep to these rules, and one draw needn't show every extreme that they name: `segment_ids`: along a row the ids never fall; each document has 1 to 768 tokens and in every row one has exactly 768. `attention_scales`: the first row lies in 0.9 to 1.6, the other two in 0.2 to 0.8.
All inputs are finite; a program needn't handle non-finite values.
Results may differ from a plain program's by a relative error of at most 0.017.
The roundings to bfloat16 on the way count: a program that leaves them out, or rounds other values in their place, can miss the bound.
Values may be sent and summed in bfloat16 or wider, within the bound.
No kernel may reach another device: no remote copies, remote signals or barrier semaphores. Data moves between devices by JAX's collectives and lax.ppermute only.
A program may use at most 320 MiB of HBM per device.

v0:
```python
import math

import jax
import jax.numpy as jnp
from jax import lax
from jax.sharding import PartitionSpec as P

HEADS = 16
HEAD_DIM = 64


norm_eps = 1e-06
neg_big = -1e30
rope_base = 10000.0
learn_rate = 0.003
beta_one = 0.9
beta_two = 0.95
adam_eps = 1e-08
corr_one = 1.0 - 0.9**10
corr_two = 1.0 - 0.95**10


def passed_along(x, axis, by):
    count = lax.axis_size(axis)
    pairs = [(i, i + by) for i in range(count) if 0 <= i + by < count]
    return lax.ppermute(x, axis, pairs)


def rms_unit(values):
    return values * lax.rsqrt(jnp.mean(values * values, axis=-1, keepdims=True) + norm_eps)


def blend(residual, branch, mixing):
    return rms_unit(residual + mixing * (rms_unit(branch) - residual))


def doc_positions(segments):
    length = segments.shape[-1]
    places = jnp.arange(length, dtype=jnp.int32)
    first_flag = jnp.ones(segments.shape[:-1] + (1,), dtype=jnp.bool_)
    change = jnp.concatenate([first_flag, segments[..., 1:] != segments[..., :-1]], axis=-1)
    starts = jnp.where(change, places, 0)
    return places - lax.cummax(starts, axis=segments.ndim - 1)


def rotate(values, positions):
    half_dim = values.shape[-1] // 2
    frequency = jnp.exp(
        jnp.arange(half_dim, dtype=jnp.float32) * (-2.0 * math.log(rope_base) / values.shape[-1])
    )
    angles = positions.astype(jnp.float32)[..., None, None] * frequency
    cosine_values = jnp.cos(angles)
    sine_values = jnp.sin(angles)
    first_half = values[..., :half_dim]
    second_half = values[..., half_dim:]
    return jnp.concatenate(
        [
            first_half * cosine_values - second_half * sine_values,
            first_half * sine_values + second_half * cosine_values,
        ],
        axis=-1,
    )


def heads_unit(projected, positions, scale_row):
    shaped = projected.reshape(projected.shape[:-1] + (HEADS, HEAD_DIM))
    turned = rotate(shaped, positions)
    unit_heads = turned * lax.rsqrt(jnp.sum(turned * turned, axis=-1, keepdims=True) + norm_eps)
    return (unit_heads * scale_row.reshape(HEADS, HEAD_DIM)).reshape(projected.shape)


def swiglu(upward, gating, up_scale, gate_scale):
    return upward * up_scale * jax.nn.silu(gating * gate_scale)


def adam_change(weight, gradient, moment_one, moment_two, renormalize):
    moment_one_new = beta_one * moment_one + (1.0 - beta_one) * gradient
    moment_two_new = beta_two * moment_two + (1.0 - beta_two) * gradient * gradient
    stepped = weight - learn_rate * (moment_one_new / corr_one) / (
        jnp.sqrt(moment_two_new / corr_two) + adam_eps
    )
    if renormalize:
        stepped = stepped * lax.rsqrt(jnp.sum(stepped * stepped, axis=-1, keepdims=True) + norm_eps)
    return stepped - weight


def head_slice(values, head):
    return lax.dynamic_slice_in_dim(values, head * HEAD_DIM, HEAD_DIM, 2)


def merge_heads(per_head):
    return jnp.moveaxis(per_head, 0, 2).reshape(per_head.shape[1], per_head.shape[2], -1)


def attend_forward(queries, key_block, value_block, allowed):
    score_gain = math.sqrt(HEAD_DIM)

    def one_head(head):
        query_head = head_slice(queries, head)
        key_head = head_slice(key_block, head)
        value_head = head_slice(value_block, head)
        scores = score_gain * jnp.einsum(
            "rqd,rkd->rqk", query_head, key_head, preferred_element_type=jnp.float32
        )
        scores = jnp.where(allowed, scores, neg_big)
        largest = jnp.max(scores, axis=-1, keepdims=True)
        exponent = jnp.exp(scores - largest)
        totals = jnp.sum(exponent, axis=-1, keepdims=True)
        probability = (exponent / totals).astype(jnp.bfloat16)
        mixed_head = jnp.einsum(
            "rqk,rkd->rqd", probability, value_head, preferred_element_type=jnp.float32
        )
        return (mixed_head, (largest + jnp.log(totals))[..., 0])

    per_head, log_sums = lax.map(one_head, jnp.arange(HEADS, dtype=jnp.int32))
    return (merge_heads(per_head), log_sums)


def attend_backward(queries, key_block, value_block, allowed, log_sums, upstream):
    score_gain = math.sqrt(HEAD_DIM)

    def one_head(head_pair):
        head, log_sum = head_pair
        query_head = head_slice(queries, head)
        key_head = head_slice(key_block, head)
        value_head = head_slice(value_block, head)
        upstream_head = head_slice(upstream, head)
        scores = score_gain * jnp.einsum(
            "rqd,rkd->rqk", query_head, key_head, preferred_element_type=jnp.float32
        )
        scores = jnp.where(allowed, scores, neg_big)
        probability = jnp.exp(scores - log_sum[..., None])
        grad_probs = jnp.einsum(
            "rqd,rkd->rqk", upstream_head, value_head, preferred_element_type=jnp.float32
        )
        grad_scores = probability * (
            grad_probs - jnp.sum(probability * grad_probs, axis=-1, keepdims=True)
        )
        grad_scores = grad_scores.astype(jnp.bfloat16)
        grad_query = score_gain * jnp.einsum(
            "rqk,rkd->rqd", grad_scores, key_head, preferred_element_type=jnp.float32
        )
        grad_key = score_gain * jnp.einsum(
            "rqk,rqd->rkd", grad_scores, query_head, preferred_element_type=jnp.float32
        )
        grad_value = jnp.einsum(
            "rqk,rqd->rkd",
            probability.astype(jnp.bfloat16),
            upstream_head,
            preferred_element_type=jnp.float32,
        )
        return (grad_query, grad_key, grad_value)

    grad_query, grad_key, grad_value = lax.map(
        one_head, (jnp.arange(HEADS, dtype=jnp.int32), log_sums)
    )
    return (merge_heads(grad_query), merge_heads(grad_key), merge_heads(grad_value))


def local(
    tokens,
    segment_ids,
    cotangent,
    attention_weights,
    feed_weights,
    attention_scales,
    feed_scales,
    attention_first,
    attention_second,
    feed_first,
    feed_second,
    attention_scale_first,
    attention_scale_second,
    feed_scale_first,
    feed_scale_second,
):
    row_count = tokens.shape[0]
    local_len = tokens.shape[1]
    token_count = row_count * local_len
    seq_rank = lax.axis_index("seq")
    offset = seq_rank * local_len
    positions = lax.dynamic_slice_in_dim(doc_positions(segment_ids), offset, local_len, 1)
    query_place = offset + jnp.arange(local_len, dtype=jnp.int32)
    key_place = offset - local_len + jnp.arange(2 * local_len, dtype=jnp.int32)
    padded_docs = jnp.concatenate(
        [jnp.full((row_count, local_len), -1, jnp.int32), segment_ids], axis=1
    )
    key_docs = lax.dynamic_slice_in_dim(padded_docs, offset, 2 * local_len, 1)
    query_docs = lax.dynamic_slice_in_dim(segment_ids, offset, local_len, 1)
    allowed = (
        (key_place[None, None, :] >= 0)
        & (key_place[None, None, :] <= query_place[None, :, None])
        & (key_docs[:, None, :] == query_docs[:, :, None])
    )
    attend_w, attend_s = (
        lax.all_gather(attention_weights.astype(jnp.bfloat16), "dp", axis=1, tiled=True),
        lax.all_gather(attention_scales.astype(jnp.bfloat16), "dp", axis=1, tiled=True),
    )
    attend_scale = attend_s.astype(jnp.float32)
    flat_tokens = tokens.reshape(token_count, -1)
    projected = jnp.einsum(
        "nd,jed->jne", flat_tokens, attend_w[:3], preferred_element_type=jnp.float32
    )

    def turn(projected_rows, scale_row):
        return heads_unit(projected_rows, positions, scale_row)

    query_unit, query_back = jax.vjp(
        turn, projected[0].reshape(row_count, local_len, -1), attend_scale[0]
    )
    key_unit, key_back = jax.vjp(
        turn, projected[1].reshape(row_count, local_len, -1), attend_scale[0]
    )
    query_round = query_unit.astype(jnp.bfloat16)
    key_round = key_unit.astype(jnp.bfloat16)
    value_round = projected[2].reshape(row_count, local_len, -1).astype(jnp.bfloat16)
    prior_keys, prior_values = passed_along((key_round, value_round), "seq", 1)
    key_block = jnp.concatenate([prior_keys, key_round], axis=1)
    value_block = jnp.concatenate([prior_values, value_round], axis=1)
    mixture, log_sums = attend_forward(query_round, key_block, value_block, allowed)
    mixture_round = mixture.reshape(token_count, -1).astype(jnp.bfloat16)
    branch = jnp.einsum("nd,de->ne", mixture_round, attend_w[3], preferred_element_type=jnp.float32)
    inputs = flat_tokens.astype(jnp.float32)
    hidden, hidden_back = jax.vjp(blend, inputs, branch, attend_scale[1])
    feed_w, feed_s = (
        lax.all_gather(feed_weights.astype(jnp.bfloat16), "dp", axis=1, tiled=True),
        lax.all_gather(feed_scales.astype(jnp.bfloat16), "dp", axis=1, tiled=True),
    )
    feed_scale = feed_s.astype(jnp.float32)
    hidden_round = hidden.astype(jnp.bfloat16)
    up_gate = jnp.einsum(
        "nd,jfd->jnf", hidden_round, feed_w[:2], preferred_element_type=jnp.float32
    )
    product, product_back = jax.vjp(swiglu, up_gate[0], up_gate[1], feed_scale[0], feed_scale[1])
    product_round = product.astype(jnp.bfloat16)
    downward = jnp.einsum("nf,fd->nd", product_round, feed_w[2], preferred_element_type=jnp.float32)
    output, output_back = jax.vjp(blend, hidden, downward, attend_scale[2])
    feed_back_w = lax.all_gather(feed_weights.astype(jnp.bfloat16), "dp", axis=1, tiled=True)
    grad_out = cotangent.reshape(token_count, -1).astype(jnp.float32)
    grad_hidden_res, grad_downward, grad_alpha_feed = output_back(grad_out)
    grad_down_round = grad_downward.astype(jnp.bfloat16)
    grad_down_w = jnp.einsum(
        "nf,nd->fd", product_round, grad_down_round, preferred_element_type=jnp.float32
    )
    grad_product = jnp.einsum(
        "nd,fd->nf", grad_down_round, feed_back_w[2], preferred_element_type=jnp.float32
    )
    grad_upward, grad_gating, grad_up_scale, grad_gate_scale = product_back(grad_product)
    grad_up_gate = jnp.stack([grad_upward, grad_gating]).astype(jnp.bfloat16)
    grad_up_gate_w = jnp.einsum(
        "jnf,nd->jfd", grad_up_gate, hidden_round, preferred_element_type=jnp.float32
    )
    grad_hidden = grad_hidden_res + jnp.einsum(
        "jnf,jfd->nd", grad_up_gate, feed_back_w[:2], preferred_element_type=jnp.float32
    )
    feed_term_w = jnp.concatenate([grad_up_gate_w, grad_down_w[None]], axis=0)
    feed_term_s = jnp.stack([grad_up_scale, grad_gate_scale])
    feed_grad_w, feed_grad_s = (
        lax.psum_scatter(feed_term_w, "dp", scatter_dimension=1, tiled=True),
        lax.psum_scatter(feed_term_s, "dp", scatter_dimension=1, tiled=True),
    )
    attend_back_w = lax.all_gather(attention_weights.astype(jnp.bfloat16), "dp", axis=1, tiled=True)
    grad_input_res, grad_branch, grad_alpha_attend = hidden_back(grad_hidden)
    grad_branch_round = grad_branch.astype(jnp.bfloat16)
    grad_out_w = jnp.einsum(
        "nd,ne->de", mixture_round, grad_branch_round, preferred_element_type=jnp.float32
    )
    grad_mixture = jnp.einsum(
        "ne,de->nd", grad_branch_round, attend_back_w[3], preferred_element_type=jnp.float32
    )
    grad_mixture = grad_mixture.astype(jnp.bfloat16).reshape(row_count, local_len, -1)
    grad_query, grad_key_block, grad_value_block = attend_backward(
        query_round, key_block, value_block, allowed, log_sums, grad_mixture
    )
    back_keys, back_values = (
        passed_along(grad_key_block[:, :local_len].astype(jnp.bfloat16), "seq", -1).astype(
            jnp.float32
        ),
        passed_along(grad_value_block[:, :local_len].astype(jnp.bfloat16), "seq", -1).astype(
            jnp.float32
        ),
    )
    grad_key = grad_key_block[:, local_len:] + back_keys
    grad_value = grad_value_block[:, local_len:] + back_values
    grad_query_raw, grad_scale_query = query_back(grad_query)
    grad_key_raw, grad_scale_key = key_back(grad_key)
    grad_projected = (
        jnp.stack([grad_query_raw, grad_key_raw, grad_value])
        .reshape(3, token_count, -1)
        .astype(jnp.bfloat16)
    )
    grad_projected_w = jnp.einsum(
        "jne,nd->jed", grad_projected, flat_tokens, preferred_element_type=jnp.float32
    )
    input_grad = grad_input_res + jnp.einsum(
        "jne,jed->nd", grad_projected, attend_back_w[:3], preferred_element_type=jnp.float32
    )
    attend_term_w = jnp.concatenate([grad_projected_w, grad_out_w[None]], axis=0)
    attend_term_s = jnp.stack(
        [grad_scale_query + grad_scale_key, grad_alpha_attend, grad_alpha_feed]
    )
    attend_grad_w, attend_grad_s = (
        lax.psum_scatter(attend_term_w, "dp", scatter_dimension=1, tiled=True),
        lax.psum_scatter(attend_term_s, "dp", scatter_dimension=1, tiled=True),
    )
    attend_grad_w, attend_grad_s, feed_grad_w, feed_grad_s = (
        lax.psum(attend_grad_w.astype(jnp.bfloat16), "seq").astype(jnp.float32),
        lax.psum(attend_grad_s.astype(jnp.bfloat16), "seq").astype(jnp.float32),
        lax.psum(feed_grad_w.astype(jnp.bfloat16), "seq").astype(jnp.float32),
        lax.psum(feed_grad_s.astype(jnp.bfloat16), "seq").astype(jnp.float32),
    )
    attention_change = adam_change(
        attention_weights, attend_grad_w, attention_first, attention_second, True
    )
    feed_change = adam_change(feed_weights, feed_grad_w, feed_first, feed_second, True)
    attention_scale_change = adam_change(
        attention_scales, attend_grad_s, attention_scale_first, attention_scale_second, False
    )
    feed_scale_change = adam_change(
        feed_scales, feed_grad_s, feed_scale_first, feed_scale_second, False
    )
    return (
        output.reshape(tokens.shape),
        input_grad.reshape(tokens.shape),
        attend_grad_w,
        feed_grad_w,
        attend_grad_s,
        feed_grad_s,
        attention_change,
        feed_change,
        attention_scale_change,
        feed_scale_change,
    )


def solution(mesh):
    placed = (
        P("dp", "seq", None),
        P("dp", None),
        P("dp", "seq", None),
        P(None, "dp", None),
        P(None, "dp", None),
        P(None, "dp"),
        P(None, "dp"),
        P(None, "dp", None),
        P(None, "dp", None),
        P(None, "dp", None),
        P(None, "dp", None),
        P(None, "dp"),
        P(None, "dp"),
        P(None, "dp"),
        P(None, "dp"),
    )
    return jax.shard_map(
        local,
        mesh=mesh,
        in_specs=placed,
        out_specs=(
            P("dp", "seq", None),
            P("dp", "seq", None),
            P(None, "dp", None),
            P(None, "dp", None),
            P(None, "dp"),
            P(None, "dp"),
            P(None, "dp", None),
            P(None, "dp", None),
            P(None, "dp"),
            P(None, "dp"),
        ),
        check_vma=False,
    )
```

profile of v0, /device:TPU:9, one launch (start us, length us, event | category | flops | bytes accessed | tf_op | source)
XLA Modules:
  0.0 2398.3 jit_solution(248052519433449107)
XLA Ops:
  13.8 27.7 %all-gather = bf16[16,64,3]{1,2,0:T(4,128)(2,1)S(1)} all-gather(bf16[1,64,3]{1,2,0:T(4,128)(2,1)S(1)} %convert_bitcast_fusion), channel_id=1, replica_groups=mesh['dp'=16,'seq'=2] {'dp'}, dimensions={0}, use_global_device_ids=true | all-gather | bytes 6528 | tf_op jit(solution)/shard_map/all_gather | solution.py:197
  42.8 80.6 %all-gather.4.cloned.1.call-done = bf16[4,1024,1024]{2,1,0:T(8,128)(2,1)} async-done(((bf16[4,64,1024]{2,1,0:T(8,128)(2,1)}), bf16[4,1024,1024]{2,1,0:T(8,128)(2,1)}) %all-gather.4.cloned.1.call-update) | async-done | bytes 8388624 | tf_op jit(solution)/shard_map/all_gather | solution.py:196
  123.4 7.3 convolution_bitcast_fusion.1
  142.0 28.3 %all_gather.17 = bf16[2,4096]{1,0:T(2,128)(2,1)S(1)} all-gather(bf16[2,256]{1,0:T(2,128)(2,1)S(1)} %convert_element_type.152), channel_id=1, replica_groups=mesh['dp'=16,'seq'=2] {'dp'}, dimensions={1}, use_global_device_ids=true | all-gather | bytes 17408 | tf_op jit(solution)/shard_map/all_gather | solution.py:227
  191.0 128.1 %while.30 = (s32[]{:T(128)}, bf16[16,1,768,64]{2,3,1,0:T(8,128)(2,1)}, f32[16,1,768]{2,1,0:T(1,128)S(1)}, s32[16]{0:T(128)S(1)}, bf16[1,768,1024]{2,1,0:T(8,128)...) while((s32[]{:T(128)}, ...), condition=%wide.region_7.8_spmd.clone.clone, body=%wide.region_4.7_spmd.clone.sunk.clone | while | flops 316144896 | bytes 15388363 | solution.py:115
  325.5 70.6 %all-gather.6.cloned.1.call-done = bf16[3,4096,1024]{2,1,0:T(8,128)(2,1)} async-done(((bf16[3,256,1024]{2,1,0:T(8,128)(2,1)}), bf16[3,4096,1024]{2,1,0:T(8,128)(2,1)}) %all-gather.6.cloned.1.call-update) | async-done | bytes 25165840 | tf_op jit(solution)/shard_map/all_gather | solution.py:226
  396.2 24.6 %fusion.57 = f32[2,768,4096]{2,1,0:T(8,128)} fusion(bf16[3,4096,1024]{2,1,0:T(8,128)(2,1)} %all-gather.6.cloned.1.call-done, f32[768,1024]{1,0:T(8,128)S(1)} %get-tuple-element.378, f32[768]{0:T(1024)S(1)} %fusion.113), kind=kOutput, calls=%fused_computation.75 | convolution fusion | flops 12886474752 | bytes 45091840 | tf_op jit(solution)/shard_map/nd,jfd->jnf/dot_general | solution.py:231
  420.7 14.9 multiply_reduce_fusion.11
  442.5 25.3 %fusion.54 = (f32[4096]{0:T(1024)}, f32[4096]{0:T(1024)}, f32[768,4096]{1,0:T(8,128)}, bf16[1,768,4096]{2,1,0:T(8,128)(2,1)}) fusion(f32[2,768,4096]{2,1,0:T(8,128)} %fusion.57, f32[4096]{0:T(1024)S(1)} %bitcast.328, f32[4096]{0:T(1024)S(1)} %bitcast.341, bf16[768,1024]{1,0:T(8,128)(2,1)S(1)} %get-tuple-element.394, ...), kind=kOutput, calls=%fused_computation.65 | convolution fusion | flops 6505357312 | bytes 54067200 | tf_op jit(solution)/shard_map/nd,fd->nf/dot_general | solution.py:245
  467.7 8.8 fusion.64
  476.6 25.4 %multiply_reduce_fusion.8 = (f32[768]{0:T(1024)S(1)}, f32[768,1024]{1,0:T(8,128)}) fusion(f32[768,1024]{1,0:T(8,128)S(1)} %get-tuple-element.378, bf16[3,4096,1024]{2,1,0:T(8,128)(2,1)} %all-gather.6.cloned.1.call-done, bf16[1,768,4096]{2,1,0:T(8,128)(2,1)} %fusion.64, bf16[1,768,4096]{2,1,0:T(8,128)(2,1)} %get-tuple-element.383, f32[1024]{0:T(1024)S(1)} %bitcast.326, ...), kind=kOutput, calls=%fused_computation.147 | convolution fusion | flops 12899843072 | bytes 40383488 | tf_op jit(solution)/shard_map/jnf,jfd->nd/dot_general | solution.py:253
  513.7 234.5 %while.31 = (s32[]{:T(128)}, f32[16,1,768,64]{2,3,1,0:T(8,128)}, f32[16,1,1536,64]{2,3,1,0:T(8,128)}, f32[16,1,1536,64]{2,3,1,0:T(8,128)}, s32[16]{0:T(128)S(1)}...) while((s32[]{:T(128)}, f32[16,1,768,64]{2,3,1,0:T(8,128)}, ...), condition=%wide.region_18.19_spmd.clone.clone, body=%wide.region_16.18_spmd.clone.sunk.clone | while | flops 770456832 | bytes 38376176 | solution.py:154
  807.4 6.3 pad_maximum_fusion.1
  813.8 22.6 fusion.60
  836.4 16.5 convolution_bitcast_fusion
  852.9 35.1 %pad_maximum_fusion = f32[3,4096,1024]{2,1,0:T(8,128)} fusion(f32[1,4096,1024]{2,1,0:T(8,128)} %convolution_bitcast_fusion, f32[2,4096,1024]{2,1,0:T(8,128)} %fusion.60), kind=kLoop, calls=%fused_computation.53 | loop fusion | flops 12582912 | bytes 100663296 | tf_op jit(solution)/shard_map/concatenate | solution.py:256
  892.0 267.9 %reduce-scatter.9.cloned.1.call-done = f32[4,64,1024]{2,1,0:T(8,128)} async-done(((f32[4,1024,1024]{2,1,0:T(8,128)}), f32[4,64,1024]{2,1,0:T(8,128)}) %reduce-scatter.9.cloned.1.call-update) | async-done | bytes 1048592 | tf_op jit(solution)/shard_map/reduce_scatter | solution.py:303
  1161.9 1027.6 %reduce-scatter.11.cloned.1.call-done = f32[3,256,1024]{2,1,0:T(8,128)} async-done(((f32[3,4096,1024]{2,1,0:T(8,128)}), f32[3,256,1024]{2,1,0:T(8,128)}) %reduce-scatter.11.cloned.1.call-update) | async-done | bytes 3145744 | tf_op jit(solution)/shard_map/reduce_scatter | solution.py:259
  2192.8 70.2 %reduce-scatter.15.cloned.1.call-done = f32[256,2]{1,0:T(8,128)} async-done(((f32[4096,2]{1,0:T(8,128)}), f32[256,2]{1,0:T(8,128)}) %reduce-scatter.15.cloned.1.call-update) | async-done | bytes 2064
  2267.5 11.4 fusion.89
  2278.9 58.9 %reduce-scatter.13.cloned.1.call-done = f32[64,3]{1,0:T(8,128)} async-done(((f32[1024,3]{1,0:T(8,128)}), f32[64,3]{1,0:T(8,128)}) %reduce-scatter.13.cloned.1.call-update) | async-done | bytes 784
  2338.7 14.0 all-reduce.5
  2353.9 22.9 all-reduce.9.cloned.1.call-done
  2380.8 7.0 multiply_reduce_fusion.1
  (494 shorter events, 487.0 us)
Async XLA Ops:
  7.2 116.2 %all-gather.4.cloned.1.call-start = ((), (), s32[]{:S(2)}) async-start(), calls=%async_computation.4 | async-start | bytes 8912896 | tf_op jit(solution)/shard_map/all_gather | solution.py:196
  9.4 114.1 %copy-start.21 = (bf16[1,768,1024]{2,1,0:T(8,128)(2,1)S(1)}, bf16[1,768,1024]{2,1,0:T(8,128)(2,1)}, u32[]{:S(2)}) copy-start(bf16[1,768,1024]{2,1,0:T(8,128)(2,1)} %param.19) | copy-start | bytes 4718596
  9.4 386.8 %all-gather.6.cloned.1.call-start = ((), (), s32[]{:S(2)}) async-start(), calls=%async_computation.5 | async-start | bytes 26738688 | tf_op jit(solution)/shard_map/all_gather | solution.py:226
  12.8 1147.0 %reduce-scatter.9.cloned.1.call-start = ((), (), s32[]{:S(2)}) async-start(), calls=%async_computation.6 | async-start | bytes 17825792 | tf_op jit(solution)/shard_map/reduce_scatter | solution.py:303
  42.4 464.5 %copy-start.48 = (f32[1,1024]{1,0:T(1,128)}, f32[1,1024]{1,0:T(1,128)S(1)}, u32[]{:S(2)}) copy-start(f32[1,1024]{1,0:T(1,128)S(1)} %get-tuple-element.407) | copy-start | bytes 12292
  42.8 91.6 %copy-start.33 = (f32[768,32]{0,1:T(8,128)}, f32[768,32]{0,1:T(8,128)S(1)}, u32[]{:S(2)}) copy-start(f32[768,32]{0,1:T(8,128)S(1)} %get-tuple-element.412) | copy-start | bytes 294916
  42.8 91.6 %copy-start.35 = (f32[768,32]{0,1:T(8,128)}, f32[768,32]{0,1:T(8,128)S(1)}, u32[]{:S(2)}) copy-start(f32[768,32]{0,1:T(8,128)S(1)} %get-tuple-element.413) | copy-start | bytes 294916
  140.5 37.7 %collective-permute-start = (bf16[1,768,1024]{1,2,0:T(8,128)(2,1)S(1)}, bf16[1,768,1024]{1,2,0:T(8,128)(2,1)}, u32[]{:S(2)}, u32[]{:S(2)}) collective-permute-start(bf16[1,768,1024]{1,2,0:T(8,128)(2,1)S(1)} %get-tuple-element.416), channel_id=1, source_target_pairs={{0,1},{2,3},{4,5},{6,7},{8,9},{10,11},{12,13},{14,15},{16,17},{18,... | collective-permute-start | bytes 4718600 | tf_op jit(solution)/shard_map/ppermute | solution.py:26
  173.5 12.6 collective-permute-start.1
  176.6 265.9 %copy-start.52 = (f32[1,4096]{1,0:T(1,128)}, f32[1,4096]{1,0:T(1,128)S(1)}, u32[]{:S(2)}) copy-start(f32[1,4096]{1,0:T(1,128)S(1)} %get-tuple-element.408) | copy-start | bytes 49156
  176.6 291.1 %copy-start.46 = (f32[1,4096]{1,0:T(1,128)}, f32[1,4096]{1,0:T(1,128)S(1)}, u32[]{:S(2)}) copy-start(f32[1,4096]{1,0:T(1,128)S(1)} %get-tuple-element.409) | copy-start | bytes 49156
  751.4 25.7 %collective-permute-start.2 = (bf16[1,768,1024]{1,2,0:T(8,128)(2,1)}, bf16[1,768,1024]{1,2,0:T(8,128)(2,1)}, u32[]{:S(2)}, u32[]{:S(2)}) collective-permute-start(bf16[1,768,1024]{1,2,0:T(8,128)(2,1)} %slice.195), channel_id=1, source_target_pairs={{1,0},{3,2},{5,4},{7,6},{9,8},{11,10},{13,12},{15,14},{17,16},{19,... | collective-permute-start | bytes 4718600 | tf_op jit(solution)/shard_map/ppermute | solution.py:26
  768.7 29.7 %collective-permute-start.3 = (bf16[1,768,1024]{2,1,0:T(8,128)(2,1)}, bf16[1,768,1024]{2,1,0:T(8,128)(2,1)}, u32[]{:S(2)}, u32[]{:S(2)}) collective-permute-start(bf16[1,768,1024]{2,1,0:T(8,128)(2,1)} %copy.103), channel_id=1, source_target_pairs={{1,0},{3,2},{5,4},{7,6},{9,8},{11,10},{13,12},{15,14},{17,16},{19,... | collective-permute-start | bytes 4718600 | tf_op jit(solution)/shard_map/ppermute | solution.py:26
  813.7 1375.7 %reduce-scatter.11.cloned.1.call-start = ((), (), s32[]{:S(2)}) async-start(), calls=%async_computation.7 | async-start | bytes 53477376 | tf_op jit(solution)/shard_map/reduce_scatter | solution.py:259
  888.0 1375.0 %reduce-scatter.15.cloned.1.call-start = ((), (), s32[]{:S(2)}) async-start(), calls=%async_computation.9 | async-start | bytes 2228224
  890.7 1447.2 %reduce-scatter.13.cloned.1.call-start = ((), (), s32[]{:S(2)}) async-start(), calls=%async_computation.8 | async-start | bytes 557056
  891.9 1484.9 %all-reduce.9.cloned.1.call-start = ((), (), s32[]{:S(2)}) async-start(), calls=%async_computation.10 | async-start | bytes 4194304 | tf_op jit(solution)/shard_map/psum | solution.py:307
  1161.9 1102.0 %copy-start.14 = (bf16[1,768,16,64]{1,3,2,0:T(8,128)(2,1)S(1)}, bf16[1,768,16,64]{1,3,2,0:T(8,128)(2,1)}, u32[]{:S(2)}) copy-start(bf16[1,768,16,64]{1,3,2,0:T(8,128)(2,1)} %add_convert_fusion.1) | copy-start | bytes 4718596
  2267.5 85.2 %copy-start.62 = (f32[3,64]{1,0:T(4,128)S(1)}, f32[3,64]{1,0:T(4,128)}, u32[]{:S(2)}) copy-start(f32[3,64]{1,0:T(4,128)} %param.24) | copy-start | bytes 2308
  2267.5 85.2 %copy-start.71 = (f32[3,64]{1,0:T(4,128)S(1)}, f32[3,64]{1,0:T(4,128)}, u32[]{:S(2)}) copy-start(f32[3,64]{1,0:T(4,128)} %param.31) | copy-start | bytes 2308
  2267.5 85.8 %copy-start.64 = (f32[2,256]{1,0:T(2,128)S(1)}, f32[2,256]{1,0:T(2,128)}, u32[]{:S(2)}) copy-start(f32[2,256]{1,0:T(2,128)} %param.25) | copy-start | bytes 6148
  2267.5 85.8 %copy-start.73 = (f32[2,256]{1,0:T(2,128)S(1)}, f32[2,256]{1,0:T(2,128)}, u32[]{:S(2)}) copy-start(f32[2,256]{1,0:T(2,128)} %param.33) | copy-start | bytes 6148
  2267.5 85.8 %copy-start.74 = (f32[2,256]{1,0:T(2,128)S(1)}, f32[2,256]{1,0:T(2,128)}, u32[]{:S(2)}) copy-start(f32[2,256]{1,0:T(2,128)} %param.32) | copy-start | bytes 6148
  2278.9 101.8 %copy-start = (f32[3,256,1024]{2,1,0:T(8,128)S(1)}, f32[3,256,1024]{2,1,0:T(8,128)}, u32[]{:S(2)}) copy-start(f32[3,256,1024]{2,1,0:T(8,128)} %param.23) | copy-start | bytes 9437188
  (62 other events, 477.0 us)
Sparse Core Ops, SparseCore 0:
  11.3 112.0 all-gather.3
  126.7 269.3 all-gather.5
  813.8 345.9 reduce-scatter.8
  1162.0 1027.3 reduce-scatter.10
  2192.2 70.7 reduce-scatter.14
  2265.6 72.1 reduce-scatter.12
  2340.9 35.8 all-reduce.8
where the time goes:
time: 2410 us; the launch traced here: 2400 us
  waiting for transfers between devices  1600 us (66%)
  matrix products  469 us (19%)
  other arithmetic  137 us (6%)
  local copies, waits for them, and re-layouts  72.4 us (3%)
  blocking collectives  70.1 us (3%)
    reduce_scatter x1, waiting for transfers between devices, local(): lax.psum_scatter(feed_term_w, 'dp', scatter_dimension=1, tiled=True)  1030 us
    reduce_scatter x1, waiting for transfers between devices, local(): lax.psum_scatter(attend_term_w, 'dp', scatter_dimension=1, tiled=True)  268 us
    unnamed x9, waiting for transfers between devices  129 us
    dot_general x32, matrix products, one_head(): jnp.einsum('rqd,rkd->rqk', query_head, key_head, preferred_element_type=j...  107 us
    all_gather x1, waiting for transfers between devices, local(): lax.all_gather(attention_weights.astype(jnp.bfloat16), 'dp', axis=1, tile...  80.6 us
    all_gather x1, waiting for transfers between devices, local(): lax.all_gather(feed_weights.astype(jnp.bfloat16), 'dp', axis=1, tiled=True)  70.6 us
  transfers between devices with their start and end apart: 11, of which 8 were waited for; matrix products, arithmetic and copies ran while one was open for 12% of the time, Pallas kernels for 0%

commit v1 on v0

v1 whole, which is shorter than its diff:
```python
import functools
import math

import jax
import jax.numpy as jnp
from jax import lax
from jax.experimental import pallas as pl
from jax.experimental.pallas import tpu as pltpu
from jax.sharding import PartitionSpec as P

HEADS = 16
HEAD_DIM = 64
PAIR = 2 * HEAD_DIM
BLOCK = 256

norm_eps = 1e-06
rope_base = 10000.0
learn_rate = 0.003
beta_one = 0.9
beta_two = 0.95
adam_eps = 1e-08
corr_one = 1.0 - 0.9**10
corr_two = 1.0 - 0.95**10
apart = 1024.0

bf16 = jnp.bfloat16
f32 = jnp.float32
NT = (((1,), (1,)), ((), ()))
NN = (((1,), (0,)), ((), ()))
TN = (((0,), (0,)), ((), ()))
MIB = 1024 * 1024


def dot(a, b, dims=NN, precision=None):
    return lax.dot_general(a, b, dims, precision=precision, preferred_element_type=f32)


def swap(x):
    return lax.ppermute(x, "seq", [(0, 1), (1, 0)])


def via(x, bits):
    count = lax.axis_size("dp")
    return lax.ppermute(x, "dp", [(i, i ^ bits) for i in range(count)])


def halves(x, axis):
    return lax.slice_in_dim(x, 0, 2, axis=axis), lax.slice_in_dim(x, 2, 4, axis=axis)


def gather_chunks(block, axis):
    own = jnp.stack([block] + [via(block, 4 * k) for k in (1, 2, 3)], axis)
    by_x = via(own, 1)
    by_y = via(own, 2)
    diagonal = jnp.concatenate([via(halves(by_y, axis)[0], 1), via(halves(by_x, axis)[1], 2)], axis)
    return [own, by_x, by_y, diagonal]


def plus(a, b):
    return (a.astype(f32) + b.astype(f32)).astype(bf16)


def reduce_chunks(chunks, axis):
    own, by_x, by_y, diagonal = chunks
    first, second = halves(diagonal, axis)
    to_y, to_x = via(first, 1), via(second, 2)
    y_first, y_second = halves(by_y, axis)
    x_first, x_second = halves(by_x, axis)
    by_y = jnp.concatenate([plus(y_first, to_y), y_second], axis)
    by_x = jnp.concatenate([x_first, plus(x_second, to_x)], axis)
    total = own.astype(f32) + via(by_x, 1).astype(f32) + via(by_y, 2).astype(f32)
    part = [lax.index_in_dim(total, k, axis, keepdims=False) for k in range(4)]
    result = part[0]
    for k in (1, 2, 3):
        result = result + via(part[k].astype(bf16), 4 * k).astype(f32)
    return result


def slot_of(offset):
    return (offset & 3) * 4 + (offset >> 2)


def offset_of(slot):
    return (slot >> 2) + 4 * (slot & 3)


def lane_index(shape):
    return lax.broadcasted_iota(jnp.int32, shape, len(shape) - 1)


def partner_lanes(x):
    low_part = (lane_index(x.shape) & 32) == 0
    return jnp.where(low_part, pltpu.roll(x, PAIR - 32, 1), pltpu.roll(x, 32, 1))


def head_sums(x):
    first = lane_index(x.shape) < HEAD_DIM
    one = jnp.sum(jnp.where(first, x, 0.0), axis=1, keepdims=True)
    two = jnp.sum(jnp.where(first, 0.0, x), axis=1, keepdims=True)
    return jnp.where(first, one, two)


def turned_unit(raw, cosine, sine):
    turned = raw * cosine + partner_lanes(raw) * sine
    scale = lax.rsqrt(head_sums(turned * turned) + norm_eps)
    return turned * scale, scale


def local_rows(block, half_blocks, rank):
    count = 2 * half_blocks
    return pl.multiple_of(lax.rem(block + half_blocks * rank, count) * BLOCK, BLOCK)


def attend_kernel(
    info, x_ref, w_ref, cos_ref, sin_ref, scale_ref, qa_ref, ka_ref,
    raw_ref, q_ref, k_ref, v_ref, mix_ref, inv_ref,
    q_aug, k_aug, p_scr,
):
    blocks = x_ref.shape[0] // BLOCK
    rank = info[blocks]
    first = lane_index((BLOCK, PAIR)) < HEAD_DIM

    def project(t, carry):
        rows = pl.ds(pl.multiple_of(t * BLOCK, BLOCK), BLOCK)
        raw = dot(x_ref[rows, :], w_ref[0], NT)
        raw_ref[rows, :] = raw[:, : 2 * PAIR]
        v_ref[rows, :] = raw[:, 2 * PAIR :].astype(bf16)
        cosine, sine = cos_ref[rows, :], sin_ref[rows, :]
        scale = scale_ref[0]
        q = (turned_unit(raw[:, :PAIR], cosine, sine)[0] * scale).astype(bf16)
        k = (turned_unit(raw[:, PAIR : 2 * PAIR], cosine, sine)[0] * scale).astype(bf16)
        q_ref[rows, :] = q
        k_ref[rows, :] = k
        q8 = q * jnp.asarray(8.0, bf16)
        qa, ka = qa_ref[rows, :], ka_ref[rows, :]
        q_aug[0, rows, :] = jnp.where(first, q8, qa)
        q_aug[1, rows, :] = jnp.where(first, qa, q8)
        k_aug[0, rows, :] = jnp.where(first, k, ka)
        k_aug[1, rows, :] = jnp.where(first, ka, k)
        return carry

    lax.fori_loop(0, blocks, project, 0)

    row = lax.broadcasted_iota(jnp.int32, (BLOCK, BLOCK), 0)
    col = lax.broadcasted_iota(jnp.int32, (BLOCK, BLOCK), 1)
    causal = col <= row
    ones = jnp.ones((8, PAIR), f32)

    def query_block(g, carry):
        q_rows = pl.ds(local_rows(g, blocks // 2, rank), BLOCK)
        count = g - info[g] + 1

        def variant(nk):
            mixed = []
            k_rows = [pl.ds(local_rows(g - (nk - 1) + j, blocks // 2, rank), BLOCK) for j in range(nk)]
            for h in range(2):
                q = q_aug[h, q_rows, :]
                lacc = None
                for j in range(nk):
                    p = jnp.exp(dot(q, k_aug[h, k_rows[j], :], NT))
                    if j == nk - 1:
                        p = jnp.where(causal, p, 0.0)
                    p_scr[h, j] = p
                    part = p[:, :PAIR] + p[:, PAIR:]
                    lacc = part if lacc is None else lacc + part
                inverse = 1.0 / jnp.sum(lacc, axis=1, keepdims=True)
                sums = dot(ones, lacc, NT, lax.Precision.HIGHEST)
                inv_ref[0, h : h + 1, q_rows] = 1.0 / sums[:1]
                acc = None
                for j in range(nk):
                    part = dot((p_scr[h, j] * inverse).astype(bf16), v_ref[k_rows[j], :])
                    acc = part if acc is None else acc + part
                mixed.append(acc)
            mix_ref[q_rows, :] = jnp.where(first, mixed[0], mixed[1]).astype(bf16)

        for nk in range(1, 5):
            pl.when(count == nk if nk < 4 else count >= 4)(functools.partial(variant, nk))
        return carry

    lax.fori_loop(0, blocks, query_block, 0)


def whole(shape):
    return pl.BlockSpec(shape, lambda p: (0,) * len(shape))


def attend_forward(info, x_all, w_pairs, cosine, sine, scale, qa, ka):
    tokens, width = x_all.shape
    pairs = w_pairs.shape[0]
    feats = pairs * PAIR
    by_pair = pl.BlockSpec((tokens, PAIR), lambda p: (0, p))
    return pl.pallas_call(
        attend_kernel,
        grid=(pairs,),
        in_specs=[
            pl.BlockSpec(memory_space=pltpu.SMEM),
            whole((tokens, width)),
            pl.BlockSpec((1, 3 * PAIR, width), lambda p: (p, 0, 0)),
            whole((tokens, PAIR)),
            whole((tokens, PAIR)),
            pl.BlockSpec((1, 1, PAIR), lambda p: (p, 0, 0)),
            whole((tokens, PAIR)),
            whole((tokens, PAIR)),
        ],
        out_specs=[
            pl.BlockSpec((tokens, 2 * PAIR), lambda p: (0, p)),
            by_pair,
            by_pair,
            by_pair,
            by_pair,
            pl.BlockSpec((1, 8, tokens), lambda p: (p, 0, 0)),
        ],
        out_shape=[
            jax.ShapeDtypeStruct((tokens, 2 * feats), f32),
            jax.ShapeDtypeStruct((tokens, feats), bf16),
            jax.ShapeDtypeStruct((tokens, feats), bf16),
            jax.ShapeDtypeStruct((tokens, feats), bf16),
            jax.ShapeDtypeStruct((tokens, feats), bf16),
            jax.ShapeDtypeStruct((pairs, 8, tokens), f32),
        ],
        scratch_shapes=[
            pltpu.VMEM((2, tokens, PAIR), bf16),
            pltpu.VMEM((2, tokens, PAIR), bf16),
            pltpu.VMEM((2, 4, BLOCK, BLOCK), f32),
        ],
        compiler_params=pltpu.CompilerParams(vmem_limit_bytes=40 * MIB),
        cost_estimate=pl.CostEstimate(flops=12_000_000_000, bytes_accessed=24_000_000, transcendentals=0),
        name="attend_forward",
    )(info, x_all, w_pairs, cosine, sine, scale, qa, ka)


def attend_back_kernel(
    info, q_ref, k_ref, v_ref, do_ref, mix_ref, inv_ref, raw_ref, cos_ref, sin_ref, scale_ref, qa_ref, ka_ref,
    grad_ref, gscale_ref,
    q_aug, k_aug, do_h, q_h, kt_h, delta, dq_acc, dk_acc, dv_acc,
):
    blocks = q_ref.shape[0] // BLOCK
    rank = info[blocks]
    first = lane_index((BLOCK, PAIR)) < HEAD_DIM
    zero = jnp.zeros((BLOCK, PAIR), bf16)
    eight = jnp.asarray(8.0, bf16)
    head_row = lax.broadcasted_iota(jnp.int32, (8, PAIR), 0)
    head_lane = lane_index((8, PAIR)) // HEAD_DIM
    head_mask = jnp.where(head_row == head_lane, 1.0, 0.0).astype(f32)

    def prepare(t, carry):
        start = pl.multiple_of(t * BLOCK, BLOCK)
        rows = pl.ds(start, BLOCK)
        q8 = q_ref[rows, :] * eight
        k = k_ref[rows, :]
        qa, ka = qa_ref[rows, :], ka_ref[rows, :]
        q_aug[0, rows, :] = jnp.where(first, q8, qa)
        q_aug[1, rows, :] = jnp.where(first, qa, q8)
        k_aug[0, rows, :] = jnp.where(first, k, ka)
        k_aug[1, rows, :] = jnp.where(first, ka, k)
        q_h[0, rows, :] = jnp.where(first, q8, zero)
        q_h[1, rows, :] = jnp.where(first, zero, q8)
        k8 = (k * eight).astype(f32)
        kt_h[0, :, rows] = jnp.where(first, k8, 0.0).T.astype(bf16)
        kt_h[1, :, rows] = jnp.where(first, 0.0, k8).T.astype(bf16)
        grad = do_ref[rows, :]
        do_h[0, rows, :] = jnp.where(first, grad, zero)
        do_h[1, rows, :] = jnp.where(first, zero, grad)
        inner = grad.astype(f32) * mix_ref[rows, :].astype(f32)
        delta[:, rows] = dot(head_mask, inner, NT, lax.Precision.HIGHEST)
        dk_acc[rows, :] = jnp.zeros((BLOCK, PAIR), f32)
        dv_acc[rows, :] = jnp.zeros((BLOCK, PAIR), f32)
        return carry

    lax.fori_loop(0, blocks, prepare, 0)

    row = lax.broadcasted_iota(jnp.int32, (BLOCK, BLOCK), 0)
    col = lax.broadcasted_iota(jnp.int32, (BLOCK, BLOCK), 1)
    causal = row <= col

    def query_block(g, carry):
        q_rows = pl.ds(local_rows(g, blocks // 2, rank), BLOCK)
        count = g - info[g] + 1

        def variant(nk):
            dq_t = None
            for j in range(nk):
                k_rows = pl.ds(local_rows(g - (nk - 1) + j, blocks // 2, rank), BLOCK)
                dk = dv = None
                for h in range(2):
                    scores = dot(k_aug[h, k_rows, :], q_aug[h, q_rows, :], NT)
                    p = jnp.exp(scores) * inv_ref[0, h : h + 1, q_rows]
                    if j == nk - 1:
                        p = jnp.where(causal, p, 0.0)
                    dp = dot(v_ref[k_rows, :], do_h[h, q_rows, :], NT)
                    ds = (p * (dp - delta[h : h + 1, q_rows])).astype(bf16)
                    dv_part = dot(p.astype(bf16), do_h[h, q_rows, :])
                    dk_part = dot(ds, q_h[h, q_rows, :])
                    dq_part = dot(kt_h[h, :, k_rows], ds)
                    dv = dv_part if dv is None else dv + dv_part
                    dk = dk_part if dk is None else dk + dk_part
                    dq_t = dq_part if dq_t is None else dq_t + dq_part
                dv_acc[k_rows, :] += dv
                dk_acc[k_rows, :] += dk
            dq_acc[q_rows, :] = dq_t.T

        for nk in range(1, 5):
            pl.when(count == nk if nk < 4 else count >= 4)(functools.partial(variant, nk))
        return carry

    lax.fori_loop(0, blocks, query_block, 0)

    def unturn(t, total):
        rows = pl.ds(pl.multiple_of(t * BLOCK, BLOCK), BLOCK)
        cosine, sine = cos_ref[rows, :], sin_ref[rows, :]
        scale = scale_ref[0]
        for which, acc in ((0, dq_acc), (1, dk_acc)):
            raw = raw_ref[rows, which * PAIR : (which + 1) * PAIR]
            unit, size = turned_unit(raw, cosine, sine)
            grad = acc[rows, :]
            total = total + jnp.sum((grad * unit).reshape(BLOCK // 8, 8, PAIR), axis=0)
            grad_unit = grad * scale
            grad_turned = size * (grad_unit - unit * head_sums(unit * grad_unit))
            grad_raw = grad_turned * cosine - partner_lanes(grad_turned) * sine
            grad_ref[rows, which * PAIR : (which + 1) * PAIR] = grad_raw.astype(bf16)
        grad_ref[rows, 2 * PAIR :] = dv_acc[rows, :].astype(bf16)
        return total

    total = lax.fori_loop(0, blocks, unturn, jnp.zeros((8, PAIR), f32))
    gscale_ref[0] = total


def attend_backward(info, q, k, v, grad_mixture, mixture, inverse, raw, cosine, sine, scale, qa, ka):
    tokens, feats = q.shape
    pairs = feats // PAIR
    by_pair = pl.BlockSpec((tokens, PAIR), lambda p: (0, p))
    half = pltpu.VMEM((2, tokens, PAIR), bf16)
    acc = pltpu.VMEM((tokens, PAIR), f32)
    return pl.pallas_call(
        attend_back_kernel,
        grid=(pairs,),
        in_specs=[
            pl.BlockSpec(memory_space=pltpu.SMEM),
            by_pair,
            by_pair,
            by_pair,
            by_pair,
            by_pair,
            pl.BlockSpec((1, 8, tokens), lambda p: (p, 0, 0)),
            pl.BlockSpec((tokens, 2 * PAIR), lambda p: (0, p)),
            whole((tokens, PAIR)),
            whole((tokens, PAIR)),
            pl.BlockSpec((1, 1, PAIR), lambda p: (p, 0, 0)),
            whole((tokens, PAIR)),
            whole((tokens, PAIR)),
        ],
        out_specs=[
            pl.BlockSpec((tokens, 3 * PAIR), lambda p: (0, p)),
            pl.BlockSpec((1, 8, PAIR), lambda p: (p, 0, 0)),
        ],
        out_shape=[
            jax.ShapeDtypeStruct((tokens, 3 * feats), bf16),
            jax.ShapeDtypeStruct((pairs, 8, PAIR), f32),
        ],
        scratch_shapes=[
            half,
            half,
            half,
            half,
            pltpu.VMEM((2, PAIR, tokens), bf16),
            pltpu.VMEM((8, tokens), f32),
            acc,
            acc,
            acc,
        ],
        compiler_params=pltpu.CompilerParams(vmem_limit_bytes=40 * MIB),
        cost_estimate=pl.CostEstimate(flops=24_000_000_000, bytes_accessed=24_000_000, transcendentals=0),
        name="attend_backward",
    )(info, q, k, v, grad_mixture, mixture, inverse, raw, cosine, sine, scale, qa, ka)


def up_gate_kernel(h_ref, w_ref, scale_ref, ug_ref, product_ref):
    units = product_ref.shape[1]
    both = dot(h_ref[...], w_ref[...], NT)
    ug_ref[...] = both.astype(bf16)
    upward = both[:, :units] * scale_ref[:, :units]
    gated = both[:, units:] * scale_ref[:, units:]
    product_ref[...] = (upward * gated / (1.0 + jnp.exp(-gated))).astype(bf16)


def tile_of(tokens):
    return 512 if tokens % 512 == 0 else 256


def up_gate(hidden, w, scale):
    tokens, width = hidden.shape
    units = w.shape[0] // 2
    tile = tile_of(tokens)
    return pl.pallas_call(
        up_gate_kernel,
        grid=(tokens // tile,),
        in_specs=[
            pl.BlockSpec((tile, width), lambda t: (t, 0)),
            whole((2 * units, width)),
            whole((1, 2 * units)),
        ],
        out_specs=[
            pl.BlockSpec((tile, 2 * units), lambda t: (t, 0)),
            pl.BlockSpec((tile, units), lambda t: (t, 0)),
        ],
        out_shape=[
            jax.ShapeDtypeStruct((tokens, 2 * units), bf16),
            jax.ShapeDtypeStruct((tokens, units), bf16),
        ],
        compiler_params=pltpu.CompilerParams(vmem_limit_bytes=32 * MIB),
        cost_estimate=pl.CostEstimate(
            flops=4 * tokens * width * units, bytes_accessed=14_000_000, transcendentals=tokens * units
        ),
        name="up_gate",
    )(hidden, w, scale)


def gate_back_kernel(grad_ref, w_ref, ug_ref, scale_ref, gug_ref, gscale_ref):
    units = w_ref.shape[0]
    grad = dot(grad_ref[...], w_ref[...], NT)
    up = ug_ref[:, :units].astype(f32)
    gate = ug_ref[:, units:].astype(f32)
    up_scale, gate_scale = scale_ref[:, :units], scale_ref[:, units:]
    gated = gate * gate_scale
    sig = 1.0 / (1.0 + jnp.exp(-gated))
    silu = gated * sig
    through = grad * silu
    grad_gated = grad * (up * up_scale) * (sig + silu * (1.0 - sig))
    gug_ref[:, :units] = (through * up_scale).astype(bf16)
    gug_ref[:, units:] = (grad_gated * gate_scale).astype(bf16)

    @pl.when(pl.program_id(0) == 0)
    def _():
        gscale_ref[...] = jnp.zeros_like(gscale_ref)

    rows = grad.shape[0] // 8
    gscale_ref[:, :units] += jnp.sum((through * up).reshape(rows, 8, units), axis=0)
    gscale_ref[:, units:] += jnp.sum((grad_gated * gate).reshape(rows, 8, units), axis=0)


def gate_back(grad, w, ug, scale):
    tokens, width = grad.shape
    units = w.shape[0]
    tile = tile_of(tokens)
    return pl.pallas_call(
        gate_back_kernel,
        grid=(tokens // tile,),
        in_specs=[
            pl.BlockSpec((tile, width), lambda t: (t, 0)),
            whole((units, width)),
            pl.BlockSpec((tile, 2 * units), lambda t: (t, 0)),
            whole((1, 2 * units)),
        ],
        out_specs=[
            pl.BlockSpec((tile, 2 * units), lambda t: (t, 0)),
            whole((8, 2 * units)),
        ],
        out_shape=[
            jax.ShapeDtypeStruct((tokens, 2 * units), bf16),
            jax.ShapeDtypeStruct((8, 2 * units), f32),
        ],
        compiler_params=pltpu.CompilerParams(vmem_limit_bytes=32 * MIB),
        cost_estimate=pl.CostEstimate(
            flops=2 * tokens * width * units, bytes_accessed=14_000_000, transcendentals=tokens * units
        ),
        name="gate_back",
    )(grad, w, ug, scale)


def sum_dots_kernel(count, *refs):
    total = dot(refs[0][...], refs[count][...])
    for c in range(1, count):
        total = total + dot(refs[c][...], refs[count + c][...])
    refs[-1][...] = total.astype(refs[-1].dtype)


def sum_dots(lefts, rights, start, rows, dtype):
    tile = 256
    depth, width = rights[0].shape
    count = len(lefts)
    return pl.pallas_call(
        functools.partial(sum_dots_kernel, count),
        grid=(rows // tile,),
        in_specs=[pl.BlockSpec((tile, depth), lambda t: (t + start // tile, 0))] * count
        + [whole((depth, width))] * count,
        out_specs=pl.BlockSpec((tile, width), lambda t: (t, 0)),
        out_shape=jax.ShapeDtypeStruct((rows, width), dtype),
        compiler_params=pltpu.CompilerParams(vmem_limit_bytes=40 * MIB),
        cost_estimate=pl.CostEstimate(
            flops=2 * rows * width * depth * count, bytes_accessed=10_000_000, transcendentals=0
        ),
        name="sum_dots",
    )(*lefts, *rights)


def rms_unit(values):
    return values * lax.rsqrt(jnp.mean(values * values, axis=-1, keepdims=True) + norm_eps)


def blend(residual, branch, mixing):
    return rms_unit(residual + mixing * (rms_unit(branch) - residual))


def adam_change(weight, gradient, moment_one, moment_two, renormalize):
    moment_one_new = beta_one * moment_one + (1.0 - beta_one) * gradient
    moment_two_new = beta_two * moment_two + (1.0 - beta_two) * gradient * gradient
    stepped = weight - learn_rate * (moment_one_new / corr_one) / (
        jnp.sqrt(moment_two_new / corr_two) + adam_eps
    )
    if renormalize:
        stepped = stepped * lax.rsqrt(jnp.sum(stepped * stepped, axis=-1, keepdims=True) + norm_eps)
    return stepped - weight


def own_half(x, rank, axis):
    size = x.shape[axis] // 2
    return lax.dynamic_slice_in_dim(x, rank * size, size, axis)


def gather_sixteen(rank, attention_weights, feed_weights, attention_scales, feed_scales):
    place = lax.axis_index("dp")
    width = attention_weights.shape[-1]
    part = own_half(attention_weights, rank, 1).astype(bf16)
    rows = part.shape[1]
    part = part.reshape(4 * rows, width)
    extra = jnp.concatenate(
        [attention_scales.reshape(-1), own_half(feed_scales, rank, 1).reshape(-1)]
    ).astype(bf16)
    used = extra.shape[0]
    extra = jnp.pad(extra[None], ((0, 7), (0, width - used)))
    chunks = gather_chunks(jnp.concatenate([part, extra], axis=0), 0)
    feed_part = own_half(feed_weights, rank, 1).astype(bf16)
    ug_chunks = gather_chunks(feed_part[:2], 1)
    d_chunks = gather_chunks(feed_part[2], 0)

    lower, upper = [], []
    for chunk in chunks:
        mine = chunk[:, : 4 * rows]
        other = swap(mine)
        lower.append(jnp.where(rank == 0, mine, other))
        upper.append(jnp.where(rank == 0, other, mine))
    shape = (HEADS, 4, rows, width)
    full = jnp.stack(
        [jnp.concatenate(lower, 0).reshape(shape), jnp.concatenate(upper, 0).reshape(shape)], 2
    )
    half = HEADS // 2
    mine = lax.dynamic_slice_in_dim(full, rank * half, half, 0)
    other = lax.dynamic_slice_in_dim(full, (1 - rank) * half, half, 0)
    w_pairs = jnp.swapaxes(mine[:, :3].reshape(half // 2, 2, 3, HEAD_DIM, width), 1, 2)
    w_pairs = w_pairs.reshape(half // 2, 3 * PAIR, width)
    wo_mine = mine[:, 3].reshape(half * HEAD_DIM, width)
    wo_other = other[:, 3].reshape(half * HEAD_DIM, width)

    extras = jnp.concatenate([chunk[:, 4 * rows] for chunk in chunks], 0)[:, :used].astype(f32)
    qk_scale = lax.dynamic_slice_in_dim(extras[:, :HEAD_DIM], rank * half, half, 0)
    alpha = jnp.take(
        extras[:, HEAD_DIM : 3 * HEAD_DIM], slot_of(jnp.arange(HEADS, dtype=jnp.int32) ^ place), axis=0
    )
    alpha = jnp.swapaxes(alpha.reshape(HEADS, 2, HEAD_DIM), 0, 1).reshape(2, width)
    feed_scale = extras[:, 3 * HEAD_DIM :].reshape(4, 4, 2, -1)
    feed = [
        (
            ug_chunks[c].reshape(-1, width),
            d_chunks[c].reshape(-1, width),
            jnp.swapaxes(feed_scale[c], 0, 1).reshape(1, -1),
        )
        for c in range(4)
    ]
    return w_pairs, wo_mine, wo_other, qk_scale.reshape(half // 2, 1, PAIR), alpha, feed


def reduce_feed_sixteen(rank, grad_ug, grad_d):
    rows = grad_d[0].shape[0] // 4
    width = grad_d[0].shape[1]
    down = reduce_chunks([g.reshape(4, rows, width) for g in grad_d], 0)
    both = reduce_chunks([g.reshape(2, 4, rows, width) for g in grad_ug], 1)
    total = jnp.concatenate([both, down[None]], 0)
    other = swap(total)
    return jnp.concatenate(
        [jnp.where(rank == 0, total, other), jnp.where(rank == 0, other, total)], 1
    )


def reduce_attend_sixteen(rank, grad_pairs, grad_wo, grad_qk, grad_alpha, grad_feed_scale):
    place = lax.axis_index("dp")
    width = grad_wo.shape[-1]
    half = HEADS // 2
    rows = HEAD_DIM // 2
    qkv = grad_pairs.reshape(half // 2, 3, 2, 2, rows, width)
    qkv = jnp.transpose(qkv, (3, 0, 2, 1, 4, 5)).reshape(2, half, 3 * rows, width)
    wo = jnp.swapaxes(grad_wo.reshape(half, 2, rows, width), 0, 1)
    both = jnp.concatenate([qkv, wo], 2)
    keep = lax.dynamic_index_in_dim(both, rank, 0, keepdims=False)
    other = swap(lax.dynamic_index_in_dim(both, 1 - rank, 0, keepdims=False))
    near = jnp.where(rank == 0, keep, other)
    far = jnp.where(rank == 0, other, keep)

    qk = jnp.zeros((HEADS, HEAD_DIM), f32)
    qk = lax.dynamic_update_slice(qk, grad_qk.reshape(half, HEAD_DIM), (rank * half, 0))
    alpha = jnp.swapaxes(grad_alpha.reshape(2, HEADS, HEAD_DIM), 0, 1).reshape(HEADS, 2 * HEAD_DIM)
    alpha = jnp.take(alpha, place ^ offset_of(jnp.arange(HEADS, dtype=jnp.int32)), axis=0)
    feed = jnp.concatenate(
        [jnp.swapaxes(g.reshape(2, 4, -1), 0, 1).reshape(4, -1) for g in grad_feed_scale], 0
    )
    extra = jnp.concatenate([qk, alpha, feed], 1).astype(bf16)
    used = extra.shape[1]
    extra = jnp.pad(extra[:, None], ((0, 0), (0, 7), (0, width - used)))
    chunks = [
        jnp.concatenate([side[at : at + 4], extra[slot : slot + 4]], 1)
        for side, at, slot in ((near, 0, 0), (near, 4, 4), (far, 0, 8), (far, 4, 12))
    ]
    total = reduce_chunks(chunks, 0)
    other = swap(total)
    low = jnp.where(rank == 0, total, other)
    high = jnp.where(rank == 0, other, total)
    grad_w = jnp.concatenate(
        [low[: 4 * rows].reshape(4, rows, width), high[: 4 * rows].reshape(4, rows, width)], 1
    )
    at = 3 * HEAD_DIM
    grad_s = (low[4 * rows, :at] + high[4 * rows, :at]).reshape(3, HEAD_DIM)
    grad_fs = jnp.concatenate(
        [low[4 * rows, at:used].reshape(2, -1), high[4 * rows, at:used].reshape(2, -1)], 1
    )
    return grad_w, grad_s, grad_fs


def gather_any(rank, attention_weights, feed_weights, attention_scales, feed_scales):
    width = attention_weights.shape[-1]
    full = lax.all_gather(attention_weights.astype(bf16), "dp", axis=1, tiled=True)
    scales = lax.all_gather(attention_scales.astype(bf16), "dp", axis=1, tiled=True).astype(f32)
    half = full.shape[1] // 2
    mine = lax.dynamic_slice_in_dim(full, rank * half, half, 1)
    pairs = half // PAIR
    w_pairs = jnp.swapaxes(mine[:3].reshape(3, pairs, PAIR, width), 0, 1).reshape(pairs, 3 * PAIR, width)
    wo_other = lax.dynamic_slice_in_dim(full[3], (1 - rank) * half, half, 0)
    qk_scale = lax.dynamic_slice_in_dim(scales[0], rank * half, half, 0)
    feed = lax.all_gather(own_half(feed_weights, rank, 1).astype(bf16), "dp", axis=1, tiled=True)
    feed_s = lax.all_gather(own_half(feed_scales, rank, 1).astype(bf16), "dp", axis=1, tiled=True)
    units = feed.shape[1] // 4
    chunks = []
    for c in range(4):
        part = feed[:, c * units : (c + 1) * units]
        scale = feed_s[:, c * units : (c + 1) * units].astype(f32)
        chunks.append((part[:2].reshape(-1, width), part[2], scale.reshape(1, -1)))
    return w_pairs, mine[3], wo_other, qk_scale.reshape(pairs, 1, PAIR), scales[1:], chunks


def reduce_feed_any(rank, grad_ug, grad_d):
    units, width = grad_d[0].shape
    parts = [
        jnp.concatenate([u.reshape(2, units, width), d[None]], 0) for u, d in zip(grad_ug, grad_d)
    ]
    total = jnp.concatenate(parts, 1)
    total = lax.psum_scatter(total, "dp", scatter_dimension=1, tiled=True).astype(f32)
    other = swap(total)
    return jnp.concatenate(
        [jnp.where(rank == 0, total, other), jnp.where(rank == 0, other, total)], 1
    )


def reduce_attend_any(rank, grad_pairs, grad_wo, grad_qk, grad_alpha, grad_feed_scale):
    pairs, width = grad_pairs.shape[0] // (3 * PAIR), grad_wo.shape[-1]
    half = pairs * PAIR
    qkv = jnp.swapaxes(grad_pairs.reshape(pairs, 3, PAIR, width), 0, 1).reshape(3, half, width)
    both = jnp.concatenate([qkv, grad_wo[None]], 0)
    full = lax.dynamic_update_slice(jnp.zeros((4, 2 * half, width), bf16), both, (0, rank * half, 0))
    total = lax.psum_scatter(full, "dp", scatter_dimension=1, tiled=True).astype(f32)
    grad_w = total + swap(total)
    qk = lax.dynamic_update_slice(jnp.zeros((1, 2 * half), f32), grad_qk.reshape(1, half), (0, rank * half))
    scales = jnp.concatenate([qk, grad_alpha], 0)
    grad_s = lax.psum_scatter(scales, "dp", scatter_dimension=1, tiled=True)
    grad_s = grad_s + swap(grad_s)
    feed = jnp.concatenate([g.reshape(2, -1) for g in grad_feed_scale], 1)
    feed = lax.psum_scatter(feed, "dp", scatter_dimension=1, tiled=True)
    other = swap(feed)
    grad_fs = jnp.concatenate(
        [jnp.where(rank == 0, feed, other), jnp.where(rank == 0, other, feed)], 1
    )
    return grad_w, grad_s, grad_fs


def local(
    tokens,
    segment_ids,
    cotangent,
    attention_weights,
    feed_weights,
    attention_scales,
    feed_scales,
    attention_first,
    attention_second,
    feed_first,
    feed_second,
    attention_scale_first,
    attention_scale_second,
    feed_scale_first,
    feed_scale_second,
):
    sixteen = lax.axis_size("dp") == HEADS
    count, width = tokens.shape[0] * tokens.shape[1], tokens.shape[-1]
    rank = lax.axis_index("seq")
    x = tokens.reshape(count, width)
    x_all = jnp.concatenate([x, swap(x)], axis=0)

    w_pairs, wo_mine, wo_other, qk_scale, alpha, feed = (gather_sixteen if sixteen else gather_any)(
        rank, attention_weights, feed_weights, attention_scales, feed_scales
    )

    segments = segment_ids.reshape(-1)
    docs = jnp.arange(8, dtype=jnp.int32)
    begins = jnp.sum((segments[None, :] < docs[:, None]).astype(jnp.int32), axis=1)
    is_doc = segments[:, None] == docs[None, :]
    starts = jnp.sum(jnp.where(is_doc, begins[None, :], 0), axis=1)
    info = jnp.concatenate([starts[::BLOCK] // BLOCK, rank[None].astype(jnp.int32)])
    place = jnp.arange(2 * count, dtype=jnp.int32)

    def arranged(values):
        own = lax.dynamic_slice_in_dim(values, rank * count, count, 0)
        other = lax.dynamic_slice_in_dim(values, (1 - rank) * count, count, 0)
        return jnp.concatenate([own, other], 0)

    positions = arranged(place - starts).astype(f32)
    frequency = jnp.exp(
        jnp.arange(HEAD_DIM // 2, dtype=f32) * (-2.0 * math.log(rope_base) / HEAD_DIM)
    )
    angles = positions[:, None] * jnp.tile(frequency, 4)[None, :]
    cosine = jnp.cos(angles)
    sign = jnp.where((jnp.arange(PAIR) & 32) == 0, -1.0, 1.0).astype(f32)
    sine = jnp.sin(angles) * sign[None, :]
    lanes = jnp.arange(PAIR, dtype=jnp.int32) & (HEAD_DIM - 1)
    own_doc = arranged(segments)[:, None] == lanes[None, :]
    query_mark = own_doc.astype(bf16)
    key_mark = jnp.where(own_doc | (lanes >= 8)[None, :], 0.0, -apart).astype(bf16)

    raw, query, key, value, mixture, inverse = attend_forward(
        info, x_all, w_pairs, cosine, sine, qk_scale, query_mark, key_mark
    )
    mixed_other = swap(mixture[count:])
    branch = dot(mixture[:count], wo_mine) + dot(mixed_other, wo_other)
    hidden, hidden_back = jax.vjp(blend, x.astype(f32), branch, alpha[0])
    hidden_round = hidden.astype(bf16)
    hidden_all = jnp.concatenate([hidden_round, swap(hidden_round)], 0)

    ugs, products = [], []
    for w_ug, _, scale in feed:
        ug, product = up_gate(hidden_all, w_ug, scale)
        ugs.append(ug)
        products.append(product)
    w_ds = [w for _, w, _ in feed]
    down_other = sum_dots(products, w_ds, count, count, bf16)
    down_own = sum_dots(products, w_ds, 0, count, f32)
    downward = down_own + swap(down_other).astype(f32)
    output, output_back = jax.vjp(blend, hidden, downward, alpha[1])

    grad_out = cotangent.reshape(count, width).astype(f32)
    grad_hidden_res, grad_downward, grad_alpha_feed = output_back(grad_out)
    grad_down_round = grad_downward.astype(bf16)
    grad_down = jnp.concatenate([grad_down_round, swap(grad_down_round)], 0)
    grad_d = [dot(product, grad_down, TN).astype(bf16) for product in products]
    gugs, grad_feed_scale = [], []
    for (w_ug, w_d, scale), ug in zip(feed, ugs):
        gug, gscale = gate_back(grad_down, w_d, ug, scale)
        gugs.append(gug)
        grad_feed_scale.append(jnp.sum(gscale, axis=0))
    grad_ug = [dot(gug, hidden_all, TN).astype(bf16) for gug in gugs]
    w_ugs = [w for w, _, _ in feed]
    back_other = sum_dots(gugs, w_ugs, count, count, bf16)
    back_own = sum_dots(gugs, w_ugs, 0, count, f32)
    grad_hidden = grad_hidden_res + back_own + swap(back_other).astype(f32)
    feed_grad = (reduce_feed_sixteen if sixteen else reduce_feed_any)(rank, grad_ug, grad_d)

    grad_input_res, grad_branch, grad_alpha_attend = hidden_back(grad_hidden)
    grad_branch_round = grad_branch.astype(bf16)
    grad_branch_all = jnp.concatenate([grad_branch_round, swap(grad_branch_round)], 0)
    grad_mixture = dot(grad_branch_all, wo_mine, NT).astype(bf16)
    grad_wo = dot(mixture, grad_branch_all, TN).astype(bf16)
    grad_qkv, grad_qk = attend_backward(
        info, query, key, value, grad_mixture, mixture, inverse, raw, cosine, sine, qk_scale, query_mark, key_mark
    )
    grad_pairs = dot(grad_qkv, x_all, TN).astype(bf16)
    w_flat = w_pairs.reshape(-1, width)
    input_other = dot(grad_qkv[count:], w_flat).astype(bf16)
    input_own = dot(grad_qkv[:count], w_flat)
    input_grad = grad_input_res + input_own + swap(input_other).astype(f32)

    attend_grad, attend_grad_s, feed_grad_s = (reduce_attend_sixteen if sixteen else reduce_attend_any)(
        rank,
        grad_pairs,
        grad_wo,
        jnp.sum(grad_qk, axis=1),
        jnp.stack([grad_alpha_attend, grad_alpha_feed]),
        grad_feed_scale,
    )
    attention_change = adam_change(
        attention_weights, attend_grad, attention_first, attention_second, True
    )
    feed_change = adam_change(feed_weights, feed_grad, feed_first, feed_second, True)
    attention_scale_change = adam_change(
        attention_scales, attend_grad_s, attention_scale_first, attention_scale_second, False
    )
    feed_scale_change = adam_change(
        feed_scales, feed_grad_s, feed_scale_first, feed_scale_second, False
    )
    return (
        output.reshape(tokens.shape),
        input_grad.reshape(tokens.shape),
        attend_grad,
        feed_grad,
        attend_grad_s,
        feed_grad_s,
        attention_change,
        feed_change,
        attention_scale_change,
        feed_scale_change,
    )


def solution(mesh):
    rows = P("dp", "seq", None)
    matrix = P(None, "dp", None)
    scale = P(None, "dp")
    return jax.shard_map(
        local,
        mesh=mesh,
        in_specs=(rows, P("dp", None), rows, matrix, matrix, scale, scale)
        + (matrix,) * 4
        + (scale,) * 4,
        out_specs=(rows, rows, matrix, matrix, scale, scale, matrix, matrix, scale, scale),
        check_vma=False,
    )
```

time: 2410 us -> 725 us (0.30)
  waiting for transfers between devices: 1600 us -> 238 us
  matrix products: 469 us -> 58.9 us
  Pallas kernels: 0 us -> 164 us
  blocking collectives: 70.1 us -> 0 us
  starting transfers between devices: 10.2 us -> 67.9 us
  other arithmetic: 137 us -> 102 us
    reduce_scatter x2 -> x0, waiting for transfers between devices: 1300 us -> none  [the longest x1 1030 us: local(): lax.psum_scatter(feed_term_w, 'dp', scatter_dimension=1, tiled=True)]
    dot_general x124 -> x15, matrix products: 469 us -> 58.9 us  [dot(): lax.dot_general(a, b, dims, precision=precision, preferred_element_type=f32)]
    ppermute x4 -> x57, waiting for transfers between devices: 2.82 us -> 238 us  [the longest x42 236 us: via(): return lax.ppermute(x, 'dp', [(i, i ^ bits) for i in range(count)])]
    pallas_call x0 -> x14, Pallas kernels: none -> 164 us  [the longest x1 56.1 us: attend_backward(): pl.pallas_call(attend_back_kernel, grid=(pairs,), in_specs=[pl.BlockSpec(...]
    all_gather x2 -> x0, waiting for transfers between devices: 151 us -> none  [the longest x1 80.6 us: local(): lax.all_gather(attention_weights.astype(jnp.bfloat16), 'dp', axis=1, tile...]
    unnamed x9 -> x0, waiting for transfers between devices: 129 us -> none
    ppermute x4 -> x57, starting transfers between devices: 9.93 us -> 67.9 us  [the longest x42 47.9 us: via(): return lax.ppermute(x, 'dp', [(i, i ^ bits) for i in range(count)])]
    all_gather x2 -> x0, blocking collectives: 56.1 us -> none  [the longest x1 28.3 us: local(): lax.all_gather(feed_scales.astype(jnp.bfloat16), 'dp', axis=1, tiled=True)]
  transfers between devices with their start and end apart: 11 -> 57, of which waited for: 8 -> 21; matrix products, arithmetic and copies ran while one was open for 12% -> 26% of each run, Pallas kernels for 0% -> 15%
where the time goes in v1:
time: 725 us; the launch traced here: 718 us
  waiting for transfers between devices  238 us (33%)
  Pallas kernels  164 us (23%)
  other arithmetic  102 us (14%)
  local copies, waits for them, and re-layouts  84 us (12%)
  starting transfers between devices  67.9 us (9%)
  matrix products  58.9 us (8%)
    ppermute x42, waiting for transfers between devices, via(): return lax.ppermute(x, 'dp', [(i, i ^ bits) for i in range(count)])  236 us
    dot_general x15, matrix products, dot(): lax.dot_general(a, b, dims, precision=precision, preferred_element_type=f32)  58.9 us
    pallas_call x1, Pallas kernels, attend_backward(): pl.pallas_call(attend_back_kernel, grid=(pairs,), in_specs=[pl.BlockSpec(...  56.1 us
    ppermute x42, starting transfers between devices, via(): return lax.ppermute(x, 'dp', [(i, i ^ bits) for i in range(count)])  47.9 us
    pallas_call x1, Pallas kernels, attend_forward(): pl.pallas_call(attend_kernel, grid=(pairs,), in_specs=[pl.BlockSpec(memor...  45 us
    unnamed x297, local copies, waits for them, and re-layouts  30.7 us
    pallas_call x4, Pallas kernels, sum_dots(): pl.pallas_call(functools.partial(sum_dots_kernel, count), grid=(rows // t...  27.6 us
    ppermute x15, starting transfers between devices, swap(): return lax.ppermute(x, 'seq', [(0, 1), (1, 0)])  19.9 us
  transfers between devices with their start and end apart: 57, of which 21 were waited for; matrix products, arithmetic and copies ran while one was open for 26% of the time, Pallas kernels for 15%

profile of v1, /device:TPU:9, one launch (start us, length us, event | category | flops | bytes accessed | tf_op | source)
XLA Modules:
  0.0 718.3 jit_solution(5513726372275317862)
XLA Ops:
  21.4 14.3 %collective-permute-done.2 = bf16[136,1024]{1,0:T(8,128)(2,1)} collective-permute-done((bf16[136,1024]{1,0:T(8,128)(2,1)S(1)}, bf16[136,1024]{1,0:T(8,128)(2,1)}, u32[]{:S(2)}, u32[]{:S(2)}) %collective-permute-start.2) | collective-permute-done | bytes 278560 | tf_op jit(solution)/shard_map/ppermute | solution.py:44
  53.4 15.7 %collective-permute-done.4 = bf16[4,136,1024]{2,0,1:T(4,128)(2,1)} collective-permute-done((bf16[4,136,1024]{2,0,1:T(4,128)(2,1)S(1)}, bf16[4,136,1024]{2,0,1:T(4,128)(2,1)}, u32[]{:S(2)}, u32[]{:S(2)}) %collective-permute-start.4) | collective-permute-done | bytes 1114144 | tf_op jit(solution)/shard_map/ppermute | solution.py:44
  85.3 6.9 collective-permute-done.6
  105.3 7.1 pad_maximum_fusion
  122.8 45.0 %attend_forward.1 = (f32[1536,1024]{1,0:T(8,128)}, bf16[1536,512]{1,0:T(8,128)(2,1)S(1)}, bf16[1536,512]{1,0:T(8,128)(2,1)S(1)}, bf16[1536,512]{1,0:T(8,128)(2,1...) custom-call(s32[7]{0:T(128)S(1)} %pad_add_fusion.1.info, ...), custom_call_target="tpu_custom_call" | custom-call | flops 12000000000 | bytes 24000000 | tf_op jit(solution)/shard_map/attend_forward/pallas_call | solution.py:192
  190.8 52.0 %collective-permute-done.18 = bf16[2,4,128,1024]{3,2,0,1:T(8,128)(2,1)} collective-permute-done((bf16[2,4,128,1024]{3,2,0,1:T(8,128)(2,1)}, bf16[2,4,128,1024]{3,2,0,1:T(8,128)(2,1)}, u32[]{:S(2)}, u32[]{:S(2)}) %collective-permute-start.18) | collective-permute-done | bytes 2097184 | tf_op jit(solution)/shard_map/ppermute | solution.py:44
  250.5 28.9 %collective-permute-done.26 = bf16[2,128,1024]{2,1,0:T(8,128)(2,1)S(1)} collective-permute-done((bf16[2,128,1024]{2,1,0:T(8,128)(2,1)S(1)}, bf16[2,128,1024]{2,1,0:T(8,128)(2,1)S(1)}, u32[]{:S(2)}, u32[]{:S(2)}) %collective-permute-start.26) | collective-permute-done | bytes 524320 | tf_op jit(solution)/shard_map/ppermute | solution.py:44
  287.5 4.5 up_gate.7
  292.0 4.5 up_gate.6
  310.7 4.8 sum_dots.5
  335.4 4.6 multiply_reduce_fusion.1
  368.9 10.3 %sum_dots.7 = bf16[768,1024]{1,0:T(8,128)(2,1)} custom-call(bf16[1536,1024]{1,0:T(8,128)(2,1)S(1)} %get-tuple-element.41.refs_0_, bf16[1536,1024]{1,0:T(8,128)(2,1)} %copy-done.38, bf16[1536,1024]{1,0:T(8,128)(2,1)} %copy-done.34, bf16[1536,1024]{1,0:T(8,128)(2,1)} %copy-done.36, bf16[1024,1024]{1,0:T(8,128)(2,1)S(1)} %bitcast.225, ...), custom_call_target="tpu_custom_call" | custom-call | flops 6442450944 | bytes 10000000 | tf_op jit(solution)/shard_map/sum_dots/pallas_call | solution.py:481
  379.2 8.7 %sum_dots.6 = f32[768,1024]{1,0:T(8,128)S(1)} custom-call(bf16[1536,1024]{1,0:T(8,128)(2,1)} %copy-done.32, bf16[1536,1024]{1,0:T(8,128)(2,1)} %copy-done.38, bf16[1536,1024]{1,0:T(8,128)(2,1)} %copy-done.34, bf16[1536,1024]{1,0:T(8,128)(2,1)} %copy-done.36, bf16[1024,1024]{1,0:T(8,128)(2,1)S(1)} %bitcast.226, bf16[1024,1024]{1,0:T(8,128)(2,1)S(1)} %bitcast.232, ...), custom_call_target="tpu_custom_call" | custom-call | flops 6442450944 | bytes 10000000 | tf_op jit(solution)/shard_map/sum_dots/pallas_call | solution.py:481
  415.8 4.7 convolution_convert_fusion.9
  428.3 4.7 convolution_convert_fusion.5
  482.1 15.7 %collective-permute-done.54 = bf16[128,1024]{1,0:T(8,128)(2,1)S(1)} collective-permute-done((bf16[128,1024]{1,0:T(8,128)(2,1)S(1)}, bf16[128,1024]{1,0:T(8,128)(2,1)S(1)}, u32[]{:S(2)}, u32[]{:S(2)}) %collective-permute-start.54) | collective-permute-done | bytes 262176 | tf_op jit(solution)/shard_map/ppermute | solution.py:44
  504.2 56.1 %attend_backward.1 = (bf16[1536,1536]{1,0:T(8,128)(2,1)}, f32[4,8,128]{2,1,0:T(8,128)S(1)}) custom-call(s32[7]{0:T(128)S(1)} %copy-done.56, bf16[1536,512]{1,0:T(8,128)(2,1)S(1)} %copy-done.58, bf16[1536,512]{1,0:T(8,128)(2,1)S(1)} %copy-done.60, bf16[1536,512]{1,0:T(8,128)(2,1)S(1)} %copy-done.62, bf16[1536,512]{1,0:T(8,128)(2,1)S(1)} %convolution_convert_fusion.1.do_ref, ...), custom_call_target="tpu_custom_call" | custom-call | flops 24000000000 | bytes 24000000 | tf_op jit(solution)/shard_map/attend_backward/pallas_call | solution.py:334
  565.6 8.3 %convolution_convert_fusion = bf16[1536,1024]{1,0:T(8,128)(2,1)S(1)} fusion(bf16[1536,1536]{1,0:T(8,128)(2,1)} %get-tuple-element.53, bf16[768,1024]{1,0:T(8,128)(2,1)} %collective-permute-done.7, bf16[768,1024]{1,0:T(8,128)(2,1)S(1)} %bitcast.250), kind=kOutput, calls=%fused_computation.21 | convolution fusion | flops 4839702528 | bytes 11010048 | tf_op jit(solution)/shard_map/dot_general | solution.py:35
  583.0 8.8 %collective-permute-start.48 = (bf16[2,128,1024]{2,1,0:T(8,128)(2,1)S(1)}, bf16[2,128,1024]{2,1,0:T(8,128)(2,1)S(1)}, u32[]{:S(2)}, u32[]{:S(2)}) collective-permute-start(bf16[2,128,1024]{2,1,0:T(8,128)(2,1)S(1)} %get-tuple-element.103), channel_id=1, source_target_pairs={{0,24},{2,26},{4,28},{6,30},{8,16},{10,18},{12,20},{14,22},{16,8},... | collective-permute-start | bytes 1572872 | tf_op jit(solution)/shard_map/ppermute | solution.py:44
  596.2 28.4 %collective-permute-done.48 = bf16[2,128,1024]{2,1,0:T(8,128)(2,1)S(1)} collective-permute-done((bf16[2,128,1024]{2,1,0:T(8,128)(2,1)S(1)}, bf16[2,128,1024]{2,1,0:T(8,128)(2,1)S(1)}, u32[]{:S(2)}, u32[]{:S(2)}) %collective-permute-start.48) | collective-permute-done | bytes 524320 | tf_op jit(solution)/shard_map/ppermute | solution.py:44
  624.6 11.2 %collective-permute-done.47 = bf16[2,128,1024]{2,1,0:T(8,128)(2,1)S(1)} collective-permute-done((bf16[2,128,1024]{2,1,0:T(8,128)(2,1)S(1)}, bf16[2,128,1024]{2,1,0:T(8,128)(2,1)S(1)}, u32[]{:S(2)}, u32[]{:S(2)}) %collective-permute-start.47) | collective-permute-done | bytes 524320 | tf_op jit(solution)/shard_map/ppermute | solution.py:44
  640.7 9.5 %collective-permute-done.36 = bf16[2,136,1024]{2,1,0:T(8,128)(2,1)S(1)} collective-permute-done((bf16[2,136,1024]{2,1,0:T(8,128)(2,1)S(1)}, bf16[2,136,1024]{2,1,0:T(8,128)(2,1)S(1)}, u32[]{:S(2)}, u32[]{:S(2)}) %collective-permute-start.36) | collective-permute-done | bytes 557088 | tf_op jit(solution)/shard_map/ppermute | solution.py:44
  661.1 16.5 %collective-permute-done.37 = bf16[4,136,1024]{2,1,0:T(8,128)(2,1)S(1)} collective-permute-done((bf16[4,136,1024]{2,1,0:T(8,128)(2,1)S(1)}, bf16[4,136,1024]{2,1,0:T(8,128)(2,1)S(1)}, u32[]{:S(2)}, u32[]{:S(2)}) %collective-permute-start.37) | collective-permute-done | bytes 1114144 | tf_op jit(solution)/shard_map/ppermute | solution.py:44
  689.4 16.6 %collective-permute-done.39 = bf16[136,1024]{1,0:T(8,128)(2,1)S(1)} collective-permute-done((bf16[136,1024]{1,0:T(8,128)(2,1)S(1)}, bf16[136,1024]{1,0:T(8,128)(2,1)S(1)}, u32[]{:S(2)}, u32[]{:S(2)}) %collective-permute-start.39) | collective-permute-done | bytes 278560 | tf_op jit(solution)/shard_map/ppermute | solution.py:44
  (591 shorter events, 327.2 us)
Async XLA Ops:
  8.6 114.0 %collective-permute-start.23 = (bf16[128,1024]{1,0:T(8,128)(2,1)}, bf16[128,1024]{1,0:T(8,128)(2,1)}, u32[]{:S(2)}, u32[]{:S(2)}) collective-permute-start(bf16[128,1024]{1,0:T(8,128)(2,1)} %get-tuple-element.134), channel_id=1, source_target_pairs={{0,24},{2,26},{4,28},{6,30},{8,16},{10,18},{12,20},{14,22},{16,8},... | collective-permute-start | bytes 786440 | tf_op jit(solution)/shard_map/ppermute | solution.py:44
  9.9 73.1 %collective-permute-start.7 = (bf16[768,1024]{1,0:T(8,128)(2,1)S(1)}, bf16[768,1024]{1,0:T(8,128)(2,1)}, u32[]{:S(2)}, u32[]{:S(2)}) collective-permute-start(bf16[768,1024]{1,0:T(8,128)(2,1)S(1)} %bitcast.248), channel_id=1, source_target_pairs={{0,1},{1,0},{2,3},{3,2},{4,5},{5,4},{6,7},{7,6},{8,9},{9,8},{10,11... | collective-permute-start | bytes 4718600 | tf_op jit(solution)/shard_map/ppermute | solution.py:39
  85.2 83.7 %collective-permute-start.22 = (bf16[128,1024]{1,0:T(8,128)(2,1)}, bf16[128,1024]{1,0:T(8,128)(2,1)}, u32[]{:S(2)}, u32[]{:S(2)}) collective-permute-start(bf16[128,1024]{1,0:T(8,128)(2,1)} %get-tuple-element.134), channel_id=1, source_target_pairs={{0,16},{2,18},{4,20},{6,22},{8,24},{10,26},{12,28},{14,30},{16,0},... | collective-permute-start | bytes 786440 | tf_op jit(solution)/shard_map/ppermute | solution.py:44
  95.7 74.0 %collective-permute-start.21 = (bf16[128,1024]{1,0:T(8,128)(2,1)}, bf16[128,1024]{1,0:T(8,128)(2,1)S(1)}, u32[]{:S(2)}, u32[]{:S(2)}) collective-permute-start(bf16[128,1024]{1,0:T(8,128)(2,1)} %get-tuple-element.134), channel_id=1, source_target_pairs={{0,8},{2,10},{4,12},{6,14},{8,0},{10,2},{12,4},{14,6},{16,24},{18,... | collective-permute-start | bytes 786440 | tf_op jit(solution)/shard_map/ppermute | solution.py:44
  98.2 75.9 %collective-permute-start.15 = (bf16[2,128,1024]{2,1,0:T(8,128)(2,1)S(1)}, bf16[2,128,1024]{2,1,0:T(8,128)(2,1)S(1)}, u32[]{:S(2)}, u32[]{:S(2)}) collective-permute-start(bf16[2,128,1024]{2,1,0:T(8,128)(2,1)S(1)} %copy-done.107), channel_id=1, source_target_pairs={{0,16},{2,18},{4,20},{6,22},{8,24},{10,26},{12,28},{14,30},{16,0},... | collective-permute-start | bytes 1572872 | tf_op jit(solution)/shard_map/ppermute | solution.py:44
  103.1 71.1 %collective-permute-start.14 = (bf16[2,128,1024]{2,1,0:T(8,128)(2,1)S(1)}, bf16[2,128,1024]{2,1,0:T(8,128)(2,1)S(1)}, u32[]{:S(2)}, u32[]{:S(2)}) collective-permute-start(bf16[2,128,1024]{2,1,0:T(8,128)(2,1)S(1)} %copy-done.107), channel_id=1, source_target_pairs={{0,8},{2,10},{4,12},{6,14},{8,0},{10,2},{12,4},{14,6},{16,24},{18,... | collective-permute-start | bytes 1572872 | tf_op jit(solution)/shard_map/ppermute | solution.py:44
  122.6 51.6 %collective-permute-start.16 = (bf16[2,128,1024]{2,1,0:T(8,128)(2,1)S(1)}, bf16[2,128,1024]{2,1,0:T(8,128)(2,1)S(1)}, u32[]{:S(2)}, u32[]{:S(2)}) collective-permute-start(bf16[2,128,1024]{2,1,0:T(8,128)(2,1)S(1)} %copy-done.107), channel_id=1, source_target_pairs={{0,24},{2,26},{4,28},{6,30},{8,16},{10,18},{12,20},{14,22},{16,8},... | collective-permute-start | bytes 1572872 | tf_op jit(solution)/shard_map/ppermute | solution.py:44
  171.3 75.5 %collective-permute-start.25 = (bf16[4,128,1024]{2,1,0:T(8,128)(2,1)S(1)}, bf16[4,128,1024]{2,1,0:T(8,128)(2,1)S(1)}, u32[]{:S(2)}, u32[]{:S(2)}) collective-permute-start(bf16[4,128,1024]{2,1,0:T(8,128)(2,1)S(1)} %pad_maximum_fusion.19), channel_id=1, source_target_pairs={{0,4},{2,6},{4,0},{6,2},{8,12},{10,14},{12,8},{14,10},{16,20},{18,... | collective-permute-start | bytes 3145736 | tf_op jit(solution)/shard_map/ppermute | solution.py:44
  174.2 74.1 %collective-permute-start.24 = (bf16[4,128,1024]{2,1,0:T(8,128)(2,1)S(1)}, bf16[4,128,1024]{2,1,0:T(8,128)(2,1)S(1)}, u32[]{:S(2)}, u32[]{:S(2)}) collective-permute-start(bf16[4,128,1024]{2,1,0:T(8,128)(2,1)S(1)} %pad_maximum_fusion.19), channel_id=1, source_target_pairs={{0,2},{2,0},{4,6},{6,4},{8,10},{10,8},{12,14},{14,12},{16,18},{18,... | collective-permute-start | bytes 3145736 | tf_op jit(solution)/shard_map/ppermute | solution.py:44
  175.8 66.9 %collective-permute-start.18 = (bf16[2,4,128,1024]{3,2,0,1:T(8,128)(2,1)}, bf16[2,4,128,1024]{3,2,0,1:T(8,128)(2,1)}, u32[]{:S(2)}, u32[]{:S(2)}) collective-permute-start(bf16[2,4,128,1024]{3,2,0,1:T(8,128)(2,1)} %pad_maximum_fusion.7), channel_id=1, source_target_pairs={{0,4},{2,6},{4,0},{6,2},{8,12},{10,14},{12,8},{14,10},{16,20},{18,... | collective-permute-start | bytes 6291464 | tf_op jit(solution)/shard_map/ppermute | solution.py:44
  176.3 68.0 %collective-permute-start.17 = (bf16[2,4,128,1024]{3,2,0,1:T(8,128)(2,1)}, bf16[2,4,128,1024]{3,2,0,1:T(8,128)(2,1)}, u32[]{:S(2)}, u32[]{:S(2)}) collective-permute-start(bf16[2,4,128,1024]{3,2,0,1:T(8,128)(2,1)} %pad_maximum_fusion.7), channel_id=1, source_target_pairs={{0,2},{2,0},{4,6},{6,4},{8,10},{10,8},{12,14},{14,12},{16,18},{18,... | collective-permute-start | bytes 6291464 | tf_op jit(solution)/shard_map/ppermute | solution.py:44
  189.8 95.5 %collective-permute-start.13 = (bf16[768,1024]{1,0:T(8,128)(2,1)S(1)}, bf16[768,1024]{1,0:T(8,128)(2,1)S(1)}, u32[]{:S(2)}, u32[]{:S(2)}) collective-permute-start(bf16[768,1024]{1,0:T(8,128)(2,1)S(1)} %multiply_convert_fusion), channel_id=1, source_target_pairs={{0,1},{1,0},{2,3},{3,2},{4,5},{5,4},{6,7},{7,6},{8,9},{9,8},{10,11... | collective-permute-start | bytes 4718600 | tf_op jit(solution)/shard_map/ppermute | solution.py:39
  244.0 40.9 %collective-permute-start.19 = (bf16[2,2,128,1024]{3,2,0,1:T(8,128)(2,1)S(1)}, bf16[2,2,128,1024]{3,2,0,1:T(8,128)(2,1)S(1)}, u32[]{:S(2)}, u32[]{:S(2)}) collective-permute-start(bf16[2,2,128,1024]{3,2,0,1:T(8,128)(2,1)S(1)} %slice.363), channel_id=1, source_target_pairs={{0,2},{2,0},{4,6},{6,4},{8,10},{10,8},{12,14},{14,12},{16,18},{18,... | collective-permute-start | bytes 3145736 | tf_op jit(solution)/shard_map/ppermute | solution.py:44
  245.6 39.4 %collective-permute-start.20 = (bf16[2,2,128,1024]{3,2,0,1:T(8,128)(2,1)S(1)}, bf16[2,2,128,1024]{3,2,0,1:T(8,128)(2,1)S(1)}, u32[]{:S(2)}, u32[]{:S(2)}) collective-permute-start(bf16[2,2,128,1024]{3,2,0,1:T(8,128)(2,1)S(1)} %slice.364), channel_id=1, source_target_pairs={{0,4},{2,6},{4,0},{6,2},{8,12},{10,14},{12,8},{14,10},{16,20},{18,... | collective-permute-start | bytes 3145736 | tf_op jit(solution)/shard_map/ppermute | solution.py:44
  392.8 51.3 %collective-permute-start.51 = (bf16[2,128,1024]{2,1,0:T(8,128)(2,1)}, bf16[2,128,1024]{2,1,0:T(8,128)(2,1)}, u32[]{:S(2)}, u32[]{:S(2)}) collective-permute-start(bf16[2,128,1024]{2,1,0:T(8,128)(2,1)} %bitcast.102), channel_id=1, source_target_pairs={{0,2},{2,0},{4,6},{6,4},{8,10},{10,8},{12,14},{14,12},{16,18},{18,... | collective-permute-start | bytes 1572872 | tf_op jit(solution)/shard_map/ppermute | solution.py:44
  394.1 46.0 %collective-permute-start.49 = (bf16[2,128,1024]{2,1,0:T(8,128)(2,1)}, bf16[2,128,1024]{2,1,0:T(8,128)(2,1)}, u32[]{:S(2)}, u32[]{:S(2)}) collective-permute-start(bf16[2,128,1024]{2,1,0:T(8,128)(2,1)} %bitcast.100), channel_id=1, source_target_pairs={{0,4},{2,6},{4,0},{6,2},{8,12},{10,14},{12,8},{14,10},{16,20},{18,... | collective-permute-start | bytes 1572872 | tf_op jit(solution)/shard_map/ppermute | solution.py:44
  414.2 46.2 %collective-permute-start.44 = (bf16[2,2,128,1024]{3,2,0,1:T(8,128)(2,1)}, bf16[2,2,128,1024]{3,2,0,1:T(8,128)(2,1)}, u32[]{:S(2)}, u32[]{:S(2)}) collective-permute-start(bf16[2,2,128,1024]{3,2,0,1:T(8,128)(2,1)} %copy.190), channel_id=1, source_target_pairs={{0,2},{2,0},{4,6},{6,4},{8,10},{10,8},{12,14},{14,12},{16,18},{18,... | collective-permute-start | bytes 3145736 | tf_op jit(solution)/shard_map/ppermute | solution.py:44
  450.4 126.6 %collective-permute-start.43 = (bf16[2,4,128,1024]{3,2,0,1:T(8,128)(2,1)}, bf16[2,4,128,1024]{3,2,0,1:T(8,128)(2,1)}, u32[]{:S(2)}, u32[]{:S(2)}) collective-permute-start(bf16[2,4,128,1024]{3,2,0,1:T(8,128)(2,1)} %pad_maximum_fusion.9), channel_id=1, source_target_pairs={{0,2},{2,0},{4,6},{6,4},{8,10},{10,8},{12,14},{14,12},{16,18},{18,... | collective-permute-start | bytes 6291464 | tf_op jit(solution)/shard_map/ppermute | solution.py:44
  459.4 40.5 %collective-permute-start.31 = (bf16[768,1024]{1,0:T(8,128)(2,1)}, bf16[768,1024]{1,0:T(8,128)(2,1)}, u32[]{:S(2)}, u32[]{:S(2)}) collective-permute-start(bf16[768,1024]{1,0:T(8,128)(2,1)} %fusion.3), channel_id=1, source_target_pairs={{0,1},{1,0},{2,3},{3,2},{4,5},{5,4},{6,7},{7,6},{8,9},{9,8},{10,11... | collective-permute-start | bytes 4718600 | tf_op jit(solution)/shard_map/ppermute | solution.py:39
  480.5 96.5 %collective-permute-start.45 = (bf16[2,4,128,1024]{3,2,0,1:T(8,128)(2,1)}, bf16[2,4,128,1024]{3,2,0,1:T(8,128)(2,1)}, u32[]{:S(2)}, u32[]{:S(2)}) collective-permute-start(bf16[2,4,128,1024]{3,2,0,1:T(8,128)(2,1)} %pad_maximum_fusion.10), channel_id=1, source_target_pairs={{0,4},{2,6},{4,0},{6,2},{8,12},{10,14},{12,8},{14,10},{16,20},{18,... | collective-permute-start | bytes 6291464 | tf_op jit(solution)/shard_map/ppermute | solution.py:44
  574.4 61.8 %collective-permute-start.33 = (bf16[8,128,1024]{2,1,0:T(8,128)(2,1)S(1)}, bf16[8,128,1024]{2,1,0:T(8,128)(2,1)S(1)}, u32[]{:S(2)}, u32[]{:S(2)}) collective-permute-start(bf16[8,128,1024]{2,1,0:T(8,128)(2,1)S(1)} %fusion.17), channel_id=1, source_target_pairs={{0,1},{1,0},{2,3},{3,2},{4,5},{5,4},{6,7},{7,6},{8,9},{9,8},{10,11... | collective-permute-start | bytes 6291464 | tf_op jit(solution)/shard_map/ppermute | solution.py:39
  583.0 41.6 %collective-permute-start.48 = (bf16[2,128,1024]{2,1,0:T(8,128)(2,1)S(1)}, bf16[2,128,1024]{2,1,0:T(8,128)(2,1)S(1)}, u32[]{:S(2)}, u32[]{:S(2)}) collective-permute-start(bf16[2,128,1024]{2,1,0:T(8,128)(2,1)S(1)} %get-tuple-element.103), channel_id=1, source_target_pairs={{0,24},{2,26},{4,28},{6,30},{8,16},{10,18},{12,20},{14,22},{16,8},... | collective-permute-start | bytes 1572872 | tf_op jit(solution)/shard_map/ppermute | solution.py:44
  591.8 44.0 %collective-permute-start.47 = (bf16[2,128,1024]{2,1,0:T(8,128)(2,1)S(1)}, bf16[2,128,1024]{2,1,0:T(8,128)(2,1)S(1)}, u32[]{:S(2)}, u32[]{:S(2)}) collective-permute-start(bf16[2,128,1024]{2,1,0:T(8,128)(2,1)S(1)} %get-tuple-element.104), channel_id=1, source_target_pairs={{0,16},{2,18},{4,20},{6,22},{8,24},{10,26},{12,28},{14,30},{16,0},... | collective-permute-start | bytes 1572872 | tf_op jit(solution)/shard_map/ppermute | solution.py:44
  594.5 61.7 %collective-permute-start.32 = (bf16[768,1024]{1,0:T(8,128)(2,1)S(1)}, bf16[768,1024]{1,0:T(8,128)(2,1)S(1)}, u32[]{:S(2)}, u32[]{:S(2)}) collective-permute-start(bf16[768,1024]{1,0:T(8,128)(2,1)S(1)} %fusion.22), channel_id=1, source_target_pairs={{0,1},{1,0},{2,3},{3,2},{4,5},{5,4},{6,7},{7,6},{8,9},{9,8},{10,11... | collective-permute-start | bytes 4718600 | tf_op jit(solution)/shard_map/ppermute | solution.py:39
  (179 other events, 1912.2 us)
